TPU v7x, 32 devices: a whole 2x2x4 slice. The times are simulated.
32 devices in a mesh: seq: 8 (over z, y), batch: 4 (over x, core).
Axes of the slice: x: 2, y: 2, z: 4, core: 2. Of those that a mesh axis runs over, the one named last changes fastest.
Arguments:
- queries: bfloat16 [4096, 4096], P(('batch', 'seq')), parts along dimension 0
- keys: bfloat16 [4096, 4096], P(('batch', 'seq')), parts along dimension 0
- values: bfloat16 [4096, 4096], P(('batch', 'seq')), parts along dimension 0, may hold values from -6 to 6
- out_grad: bfloat16 [4096, 4096], P(('batch', 'seq')), parts along dimension 0, may hold values from -6 to 6
- key_blocks: int32 [128, 16, 12], P('batch'), parts along dimension 0, may hold values from -1 to 15, as said below
- dilation: int32 [128], P('batch'), parts along dimension 0, may hold values from 1 to 729, as said below
Outputs:
- attended: bfloat16 [4096, 4096], P(('batch', 'seq')), parts along dimension 0
- queries_grad: bfloat16 [4096, 4096], P(('batch', 'seq')), parts along dimension 0
- keys_grad: bfloat16 [4096, 4096], P(('batch', 'seq')), parts along dimension 0
- values_grad: bfloat16 [4096, 4096], P(('batch', 'seq')), parts along dimension 0
There are 4 independent parts, one for each index of `batch`. A program takes and returns all parts, laid end to end along the dimension named above; each array names one. Nothing has to cross between parts.
Inputs may be any that keep to these rules, and one draw needn't show every extreme that they name: `key_blocks`: in every row the first entry is the query block itself; the listed blocks are distinct, not after the query block, and stand before the -1 entries. Some head lists 12 blocks for each of its last query blocks. `dilation`: every value is a power of three.
All inputs are finite; a program needn't handle non-finite values.
Results may differ from a plain program's by a relative error of at most 0.012.
Values may be sent and summed in bfloat16 or wider, within the bound.
A program may use at most 64 MiB of HBM per device.

v0:
```python
import math

import jax
import jax.numpy as jnp
from jax import lax
from jax.sharding import PartitionSpec as P

HEADS = 32
HEAD_DIM = 128
BLOCK = 64


very_low = -1e30


def tile_mask(group_ids, chosen, valid, spacing, block_size):
    offsets = lax.broadcasted_iota(jnp.int32, (block_size, block_size), 0) - lax.broadcasted_iota(
        jnp.int32, (block_size, block_size), 1
    )
    distance = ((group_ids[:, None] - chosen) * block_size)[:, None, :, None] + offsets[
        None, :, None, :
    ]
    allowed = valid[:, None, :, None] & (distance >= 0) & (distance % spacing == 0)
    return allowed.reshape(allowed.shape[0], block_size, chosen.shape[1] * block_size)


def group_scores(query_tile, key_rows, lists, group_ids, spacing, score_scale):
    group_size, block_size, head_size = query_tile.shape
    valid = lists >= 0
    chosen = jnp.maximum(lists, 0)
    keys_tile = key_rows[chosen].reshape(group_size, -1, head_size)
    allowed = tile_mask(group_ids, chosen, valid, spacing, block_size)
    raw_scores = (
        jnp.einsum("gae,gke->gak", query_tile, keys_tile, preferred_element_type=jnp.float32)
        * score_scale
    )
    return (chosen, keys_tile, jnp.where(allowed, raw_scores, very_low))


def grouped(array, group_size):
    return array.reshape((array.shape[0] // group_size, group_size) + array.shape[1:])


def head_forward(query_rows, key_rows, value_rows, block_rows, spacing, score_scale):
    number_rows, block_size, head_size = query_rows.shape
    group_size = min(512 // block_size, number_rows)
    all_ids = jnp.arange(number_rows, dtype=jnp.int32)

    def one_group(operands):
        query_tile, lists, group_ids = operands
        chosen, keys_tile, scores = group_scores(
            query_tile, key_rows, lists, group_ids, spacing, score_scale
        )
        row_top = jnp.max(scores, axis=2)
        expos = jnp.exp(scores - row_top[:, :, None])
        row_total = jnp.sum(expos, axis=2)
        weights = expos / row_total[:, :, None]
        values_tile = value_rows[chosen].reshape(query_tile.shape[0], -1, head_size)
        output_tile = jnp.einsum(
            "gak,gke->gae",
            weights.astype(jnp.bfloat16),
            values_tile,
            preferred_element_type=jnp.float32,
        ).astype(jnp.bfloat16)
        return (output_tile, row_top, row_total)

    outputs, tops, totals = lax.map(
        one_group,
        (
            grouped(query_rows, group_size),
            grouped(block_rows, group_size),
            grouped(all_ids, group_size),
        ),
    )
    return (
        outputs.reshape(query_rows.shape),
        tops.reshape(number_rows, block_size),
        totals.reshape(number_rows, block_size),
    )


def head_backward(
    query_rows,
    grad_rows,
    key_rows,
    value_rows,
    output_rows,
    tops,
    totals,
    block_rows,
    spacing,
    score_scale,
):
    number_rows, block_size, head_size = query_rows.shape
    group_size = min(512 // block_size, number_rows)
    all_ids = jnp.arange(number_rows, dtype=jnp.int32)

    def one_group(carried, operands):
        keys_sum, values_sum = carried
        query_tile, grad_tile, output_tile, row_top, row_total, lists, group_ids = operands
        chosen, keys_tile, scores = group_scores(
            query_tile, key_rows, lists, group_ids, spacing, score_scale
        )
        weights = jnp.exp(scores - row_top[:, :, None]) / row_total[:, :, None]
        weights16 = weights.astype(jnp.bfloat16)
        values_tile = value_rows[chosen].reshape(query_tile.shape[0], -1, head_size)
        delta = jnp.sum(grad_tile.astype(jnp.float32) * output_tile.astype(jnp.float32), axis=2)
        values_part = jnp.einsum(
            "gak,gae->gke", weights16, grad_tile, preferred_element_type=jnp.float32
        ).reshape(-1, block_size, head_size)
        dweights = jnp.einsum(
            "gae,gke->gak", grad_tile, values_tile, preferred_element_type=jnp.float32
        )
        dscores16 = (weights * (dweights - delta[:, :, None])).astype(jnp.bfloat16)
        query_part = (
            jnp.einsum("gak,gke->gae", dscores16, keys_tile, preferred_element_type=jnp.float32)
            * score_scale
        ).astype(jnp.bfloat16)
        keys_part = (
            jnp.einsum("gak,gae->gke", dscores16, query_tile, preferred_element_type=jnp.float32)
            * score_scale
        ).reshape(-1, block_size, head_size)
        flat_ids = chosen.reshape(-1)
        return (
            (keys_sum.at[flat_ids].add(keys_part), values_sum.at[flat_ids].add(values_part)),
            query_part,
        )

    zeros_start = jnp.zeros(key_rows.shape, jnp.float32)
    operands = (
        grouped(query_rows, group_size),
        grouped(grad_rows, group_size),
        grouped(output_rows, group_size),
        grouped(tops, group_size),
        grouped(totals, group_size),
        grouped(block_rows, group_size),
        grouped(all_ids, group_size),
    )
    (keys_sum, values_sum), query_parts = lax.scan(one_group, (zeros_start, zeros_start), operands)
    return (
        query_parts.reshape(query_rows.shape),
        keys_sum.astype(jnp.bfloat16),
        values_sum.astype(jnp.bfloat16),
    )


def head_columns(rows, local_head, head_size):
    return lax.slice_in_dim(rows, local_head * head_size, (local_head + 1) * head_size, axis=2)


def head_lists(key_blocks, dilation, head_index):
    block_rows = lax.dynamic_index_in_dim(key_blocks, head_index, 0, keepdims=False)
    spacing = lax.dynamic_index_in_dim(dilation, head_index, 0, keepdims=False)
    return (block_rows, spacing)


def forward_all(
    blocked_queries,
    blocked_keys,
    blocked_values,
    key_blocks,
    dilation,
    my_index,
    local_heads,
    score_scale,
):
    outputs, stats = ([], [])
    for local_head in range(local_heads):
        block_rows, spacing = head_lists(key_blocks, dilation, my_index * local_heads + local_head)
        output_rows, tops, totals = head_forward(
            head_columns(blocked_queries, local_head, HEAD_DIM),
            head_columns(blocked_keys, local_head, HEAD_DIM),
            head_columns(blocked_values, local_head, HEAD_DIM),
            block_rows,
            spacing,
            score_scale,
        )
        outputs.append(output_rows)
        stats.append((tops, totals))
    return (outputs, stats)


def backward_all(
    blocked_queries,
    blocked_grads,
    blocked_keys,
    blocked_values,
    outputs,
    stats,
    key_blocks,
    dilation,
    my_index,
    local_heads,
    score_scale,
):
    collected = ([], [], [])
    for local_head in range(local_heads):
        block_rows, spacing = head_lists(key_blocks, dilation, my_index * local_heads + local_head)
        results = head_backward(
            head_columns(blocked_queries, local_head, HEAD_DIM),
            head_columns(blocked_grads, local_head, HEAD_DIM),
            head_columns(blocked_keys, local_head, HEAD_DIM),
            head_columns(blocked_values, local_head, HEAD_DIM),
            outputs[local_head],
            stats[local_head][0],
            stats[local_head][1],
            block_rows,
            spacing,
            score_scale,
        )
        for bucket, result in zip(collected, results):
            bucket.append(result)
    return tuple((jnp.concatenate(bucket, axis=2) for bucket in collected))


def blocked_form(rows):
    return rows.reshape(rows.shape[0] // BLOCK, BLOCK, rows.shape[1])


def local(queries, keys, values, out_grad, key_blocks, dilation):
    devices = lax.axis_size("seq")
    my_index = lax.axis_index("seq")
    local_heads = HEADS // devices
    score_scale = 1.0 / math.sqrt(HEAD_DIM)
    heads_queries, heads_keys, heads_values, heads_grads = (
        lax.all_to_all(queries, "seq", split_axis=1, concat_axis=0, tiled=True),
        lax.all_to_all(keys, "seq", split_axis=1, concat_axis=0, tiled=True),
        lax.all_to_all(values, "seq", split_axis=1, concat_axis=0, tiled=True),
        lax.all_to_all(out_grad, "seq", split_axis=1, concat_axis=0, tiled=True),
    )
    seq_len, width_local = heads_queries.shape
    blocked_queries = blocked_form(heads_queries)
    blocked_keys = blocked_form(heads_keys)
    blocked_values = blocked_form(heads_values)
    outputs, stats = forward_all(
        blocked_queries,
        blocked_keys,
        blocked_values,
        key_blocks,
        dilation,
        my_index,
        local_heads,
        score_scale,
    )
    queries_grad, keys_grad, values_grad = backward_all(
        blocked_queries,
        blocked_form(heads_grads),
        blocked_keys,
        blocked_values,
        outputs,
        stats,
        key_blocks,
        dilation,
        my_index,
        local_heads,
        score_scale,
    )
    attended = jnp.concatenate(outputs, axis=2).reshape(seq_len, width_local)
    return (
        lax.all_to_all(attended, "seq", split_axis=0, concat_axis=1, tiled=True),
        lax.all_to_all(
            queries_grad.reshape(seq_len, width_local),
            "seq",
            split_axis=0,
            concat_axis=1,
            tiled=True,
        ),
        lax.all_to_all(
            keys_grad.reshape(seq_len, width_local), "seq", split_axis=0, concat_axis=1, tiled=True
        ),
        lax.all_to_all(
            values_grad.reshape(seq_len, width_local),
            "seq",
            split_axis=0,
            concat_axis=1,
            tiled=True,
        ),
    )


def solution(mesh):
    return jax.shard_map(
        local,
        mesh=mesh,
        in_specs=(
            P(("batch", "seq"), None),
            P(("batch", "seq"), None),
            P(("batch", "seq"), None),
            P(("batch", "seq"), None),
            P("batch", None, None),
            P("batch"),
        ),
        out_specs=(
            P(("batch", "seq"), None),
            P(("batch", "seq"), None),
            P(("batch", "seq"), None),
            P(("batch", "seq"), None),
        ),
        check_vma=False,
    )
```

profile of v0, /device:TPU:0, one launch (start us, length us, event | category | flops | bytes accessed | tf_op | source)
XLA Modules:
  0.0 895.0 jit_solution(1589426814138803823)
XLA Ops:
  12.1 24.7 %all-to-all-done = bf16[128,8,512]{2,0,1:T(8,128)(2,1)S(1)} async-done(((bf16[128,8,512]{2,0,1:T(8,128)(2,1)}), bf16[128,8,512]{2,0,1:T(8,128)(2,1)S(1)}, u32[]{:S(2)}, u32[]{:S(2)}) %all-to-all-start) | async-done | bytes 1048608 | tf_op jit(solution)/shard_map/all_to_all | solution.py:226
  41.4 24.9 %all-to-all-done.1 = bf16[128,8,512]{2,0,1:T(8,128)(2,1)S(1)} async-done(((bf16[128,8,512]{2,0,1:T(8,128)(2,1)}), bf16[128,8,512]{2,0,1:T(8,128)(2,1)S(1)}, u32[]{:S(2)}, u32[]{:S(2)}) %all-to-all-start.1) | async-done | bytes 1048608 | tf_op jit(solution)/shard_map/all_to_all | solution.py:227
  101.3 49.9 %while.128 = (s32[]{:T(128)}, bf16[2,8,64,128]{3,2,1,0:T(8,128)(2,1)S(1)}, f32[2,8,64]{2,1,0:T(8,128)S(1)}, f32[2,8,64]{2,1,0:T(8,128)S(1)}, s32[2,8,12]{2,1,0:T...) while((s32[]{:T(128)}, ...), condition=%wide.region_3.4_spmd, body=%wide.region_0.3_spmd.sunk | while | flops 209260928 | bytes 27983584 | solution.py:67
  103.9 17.0 %fusion.301 = (f32[8,64]{1,0:T(8,128)S(1)}, f32[8,64,768]{2,1,0:T(8,128)S(1)}) fusion(bf16[8,768,128]{2,1,0:T(8,128)(2,1)S(1)} %bitcast.576, bf16[2,8,64,128]{3,2,1,0:T(8,128)(2,1)} %get-tuple-element.2324, s32[]{:T(128)} %get-tuple-element.2304, pred[]{:T(512)} %get-tuple-element.2323, s32[]{:T(128)} %get-tuple-element.2322, s32[64,768]{1,0:T(8,128)} %add.740, ...), kind=kOutput, calls=%fused_computation.331.clone.1 | convolution fusion | flops 106561024 | bytes 3507712 | tf_op jit(solution)/shard_map/while/body/eval_jaxpr/gae,gke->gak/dot_general | solution.py:34
  128.7 17.0 %fusion.301 = (f32[8,64]{1,0:T(8,128)S(1)}, f32[8,64,768]{2,1,0:T(8,128)S(1)}) fusion(bf16[8,768,128]{2,1,0:T(8,128)(2,1)S(1)} %bitcast.576, bf16[2,8,64,128]{3,2,1,0:T(8,128)(2,1)} %get-tuple-element.2324, s32[]{:T(128)} %get-tuple-element.2304, pred[]{:T(512)} %get-tuple-element.2323, s32[]{:T(128)} %get-tuple-element.2322, s32[64,768]{1,0:T(8,128)} %add.740, ...), kind=kOutput, calls=%fused_computation.331.clone.1 | convolution fusion | flops 106561024 | bytes 3507712 | tf_op jit(solution)/shard_map/while/body/eval_jaxpr/gae,gke->gak/dot_general | solution.py:34
  154.9 137.0 %while.132 = (s32[]{:T(128)}, f32[16,64,128]{2,1,0:T(8,128)S(1)}, f32[16,64,128]{2,1,0:T(8,128)S(1)}, bf16[2,8,64,128]{3,2,1,0:T(8,128)(2,1)}, s32[2,8,12]{2,1,0...) while((s32[]{:T(128)}, f32[16,64,128]{2,1,0:T(8,128)S(1)}, ...), condition=%wide.region_20.21_spmd, body=%wide.region_16.20_spmd.sunk | while | flops 513938304 | bytes 52483084 | solution.py:139
  171.9 18.7 %exponential_divide_fusion.8 = f32[8,64,768]{2,1,0:T(8,128)} fusion(bf16[8,768,128]{2,1,0:T(8,128)(2,1)} %bitcast.568, f32[8,64]{1,0:T(8,128)S(1)} %get-tuple-element.2124, f32[8,64]{1,0:T(8,128)S(1)} %get-tuple-element.2125, s32[]{:T(128)} %get-tuple-element.2510, s32[64,768]{1,0:T(8,128)S(1)} %add.764, s32[8,768]{1,0:T(8,128)S(1)} %add.766, ...), kind=kOutput, calls=%fused_computation.156.clone.1 | convolution fusion | flops 106954752 | bytes 3509760 | tf_op jit(solution)/shard_map/while/body/eval_jaxpr/gae,gke->gak/dot_general | solution.py:34
  226.8 18.7 %exponential_divide_fusion.8 = f32[8,64,768]{2,1,0:T(8,128)} fusion(bf16[8,768,128]{2,1,0:T(8,128)(2,1)} %bitcast.568, f32[8,64]{1,0:T(8,128)S(1)} %get-tuple-element.2124, f32[8,64]{1,0:T(8,128)S(1)} %get-tuple-element.2125, s32[]{:T(128)} %get-tuple-element.2510, s32[64,768]{1,0:T(8,128)S(1)} %add.764, s32[8,768]{1,0:T(8,128)S(1)} %add.766, ...), kind=kOutput, calls=%fused_computation.156.clone.1 | convolution fusion | flops 106954752 | bytes 3509760 | tf_op jit(solution)/shard_map/while/body/eval_jaxpr/gae,gke->gak/dot_general | solution.py:34
  293.5 49.9 %while.129 = (s32[]{:T(128)}, bf16[2,8,64,128]{3,2,1,0:T(8,128)(2,1)}, f32[2,8,64]{2,1,0:T(8,128)S(1)}, f32[2,8,64]{2,1,0:T(8,128)S(1)}, s32[2,8,12]{2,1,0:T(8,1...) while((s32[]{:T(128)}, ...), condition=%wide.region_7.8_spmd, body=%wide.region_4.7_spmd.sunk | while | flops 209260928 | bytes 30080792 | solution.py:67
  344.3 106.5 %while.133 = (s32[]{:T(128)}, f32[16,64,128]{2,1,0:T(8,128)S(1)}, f32[16,64,128]{2,1,0:T(8,128)S(1)}, bf16[2,8,64,128]{3,2,1,0:T(8,128)(2,1)}, s32[2,8,12]{2,1,0...) while((s32[]{:T(128)}, f32[16,64,128]{2,1,0:T(8,128)S(1)}, ...), condition=%wide.region_25.26_spmd, body=%wide.region_21.25_spmd.sunk | while | flops 513938304 | bytes 56679560 | solution.py:139
  347.0 18.6 %exponential_divide_fusion.9 = f32[8,64,768]{2,1,0:T(8,128)} fusion(bf16[8,768,128]{2,1,0:T(8,128)(2,1)} %bitcast.570, f32[8,64]{1,0:T(8,128)S(1)} %get-tuple-element.2143, f32[8,64]{1,0:T(8,128)S(1)} %get-tuple-element.2144, s32[]{:T(128)} %get-tuple-element.2462, s32[64,768]{1,0:T(8,128)S(1)} %add.773, s32[8,768]{1,0:T(8,128)S(1)} %add.775, ...), kind=kOutput, calls=%fused_computation.199.clone.1 | convolution fusion | flops 106954752 | bytes 3512329 | tf_op jit(solution)/shard_map/while/body/eval_jaxpr/gae,gke->gak/dot_general | solution.py:34
  400.3 18.6 %exponential_divide_fusion.9 = f32[8,64,768]{2,1,0:T(8,128)} fusion(bf16[8,768,128]{2,1,0:T(8,128)(2,1)} %bitcast.570, f32[8,64]{1,0:T(8,128)S(1)} %get-tuple-element.2143, f32[8,64]{1,0:T(8,128)S(1)} %get-tuple-element.2144, s32[]{:T(128)} %get-tuple-element.2462, s32[64,768]{1,0:T(8,128)S(1)} %add.773, s32[8,768]{1,0:T(8,128)S(1)} %add.775, ...), kind=kOutput, calls=%fused_computation.199.clone.1 | convolution fusion | flops 106954752 | bytes 3512329 | tf_op jit(solution)/shard_map/while/body/eval_jaxpr/gae,gke->gak/dot_general | solution.py:34
  452.5 50.0 %while.130 = (s32[]{:T(128)}, bf16[2,8,64,128]{3,2,1,0:T(8,128)(2,1)}, f32[2,8,64]{2,1,0:T(8,128)S(1)}, f32[2,8,64]{2,1,0:T(8,128)S(1)}, s32[2,8,12]{2,1,0:T(8,1...) while((s32[]{:T(128)}, ...), condition=%wide.region_11.12_spmd, body=%wide.region_8.11_spmd.sunk | while | flops 209260928 | bytes 30080792 | solution.py:67
  503.4 106.5 %while.134 = (s32[]{:T(128)}, f32[16,64,128]{2,1,0:T(8,128)S(1)}, f32[16,64,128]{2,1,0:T(8,128)S(1)}, bf16[2,8,64,128]{3,2,1,0:T(8,128)(2,1)}, s32[2,8,12]{2,1,0...) while((s32[]{:T(128)}, f32[16,64,128]{2,1,0:T(8,128)S(1)}, ...), condition=%wide.region_30.31_spmd, body=%wide.region_26.30_spmd.sunk | while | flops 513938304 | bytes 56679560 | solution.py:139
  506.1 18.6 %exponential_divide_fusion.10 = f32[8,64,768]{2,1,0:T(8,128)} fusion(bf16[8,768,128]{2,1,0:T(8,128)(2,1)} %bitcast.572, f32[8,64]{1,0:T(8,128)S(1)} %get-tuple-element.2162, f32[8,64]{1,0:T(8,128)S(1)} %get-tuple-element.2163, s32[]{:T(128)} %get-tuple-element.2414, s32[64,768]{1,0:T(8,128)S(1)} %add.782, s32[8,768]{1,0:T(8,128)S(1)} %add.784, ...), kind=kOutput, calls=%fused_computation.242.clone.1 | convolution fusion | flops 106954752 | bytes 3512329 | tf_op jit(solution)/shard_map/while/body/eval_jaxpr/gae,gke->gak/dot_general | solution.py:34
  559.4 18.6 %exponential_divide_fusion.10 = f32[8,64,768]{2,1,0:T(8,128)} fusion(bf16[8,768,128]{2,1,0:T(8,128)(2,1)} %bitcast.572, f32[8,64]{1,0:T(8,128)S(1)} %get-tuple-element.2162, f32[8,64]{1,0:T(8,128)S(1)} %get-tuple-element.2163, s32[]{:T(128)} %get-tuple-element.2414, s32[64,768]{1,0:T(8,128)S(1)} %add.782, s32[8,768]{1,0:T(8,128)S(1)} %add.784, ...), kind=kOutput, calls=%fused_computation.242.clone.1 | convolution fusion | flops 106954752 | bytes 3512329 | tf_op jit(solution)/shard_map/while/body/eval_jaxpr/gae,gke->gak/dot_general | solution.py:34
  611.4 51.4 %while.131 = (s32[]{:T(128)}, bf16[2,8,64,128]{3,2,1,0:T(8,128)(2,1)}, f32[2,8,64]{2,1,0:T(8,128)S(1)}, f32[2,8,64]{2,1,0:T(8,128)S(1)}, s32[2,8,12]{2,1,0:T(8,1...) while((s32[]{:T(128)}, ...), condition=%wide.region_15.16_spmd, body=%wide.region_12.15_spmd.sunk | while | flops 209260928 | bytes 30080792 | solution.py:67
  663.7 106.8 %while.135 = (s32[]{:T(128)}, f32[16,64,128]{2,1,0:T(8,128)S(1)}, f32[16,64,128]{2,1,0:T(8,128)S(1)}, bf16[2,8,64,128]{3,2,1,0:T(8,128)(2,1)}, s32[2,8,12]{2,1,0...) while((s32[]{:T(128)}, f32[16,64,128]{2,1,0:T(8,128)S(1)}, ...), condition=%wide.region_35.36_spmd, body=%wide.region_31.35_spmd.sunk | while | flops 513938304 | bytes 56679560 | solution.py:139
  666.4 18.6 %exponential_divide_fusion.11 = f32[8,64,768]{2,1,0:T(8,128)} fusion(bf16[8,768,128]{2,1,0:T(8,128)(2,1)} %bitcast.574, f32[8,64]{1,0:T(8,128)S(1)} %get-tuple-element.2181, f32[8,64]{1,0:T(8,128)S(1)} %get-tuple-element.2182, s32[]{:T(128)} %get-tuple-element.2366, s32[64,768]{1,0:T(8,128)S(1)} %add.791, s32[8,768]{1,0:T(8,128)S(1)} %add.793, ...), kind=kOutput, calls=%fused_computation.285.clone.1 | convolution fusion | flops 106954752 | bytes 3512329 | tf_op jit(solution)/shard_map/while/body/eval_jaxpr/gae,gke->gak/dot_general | solution.py:34
  719.7 18.6 %exponential_divide_fusion.11 = f32[8,64,768]{2,1,0:T(8,128)} fusion(bf16[8,768,128]{2,1,0:T(8,128)(2,1)} %bitcast.574, f32[8,64]{1,0:T(8,128)S(1)} %get-tuple-element.2181, f32[8,64]{1,0:T(8,128)S(1)} %get-tuple-element.2182, s32[]{:T(128)} %get-tuple-element.2366, s32[64,768]{1,0:T(8,128)S(1)} %add.791, s32[8,768]{1,0:T(8,128)S(1)} %add.793, ...), kind=kOutput, calls=%fused_computation.285.clone.1 | convolution fusion | flops 106954752 | bytes 3512329 | tf_op jit(solution)/shard_map/while/body/eval_jaxpr/gae,gke->gak/dot_general | solution.py:34
  780.0 24.0 %all-to-all-done.7 = bf16[8,128,512]{2,1,0:T(8,128)(2,1)S(1)} async-done(((bf16[8,128,512]{2,1,0:T(8,128)(2,1)}), bf16[8,128,512]{2,1,0:T(8,128)(2,1)S(1)}, u32[]{:S(2)}, u32[]{:S(2)}) %all-to-all-start.7) | async-done | bytes 1048608 | tf_op jit(solution)/shard_map/all_to_all | solution.py:271
  808.7 24.6 %all-to-all-done.6 = bf16[8,128,512]{2,1,0:T(8,128)(2,1)S(1)} async-done(((bf16[8,128,512]{2,1,0:T(8,128)(2,1)}), bf16[8,128,512]{2,1,0:T(8,128)(2,1)S(1)}, u32[]{:S(2)}, u32[]{:S(2)}) %all-to-all-start.6) | async-done | bytes 1048608 | tf_op jit(solution)/shard_map/all_to_all | solution.py:268
  838.7 24.5 %all-to-all-done.5 = bf16[8,128,512]{2,1,0:T(8,128)(2,1)} async-done(((bf16[8,128,512]{2,1,0:T(8,128)(2,1)}), bf16[8,128,512]{2,1,0:T(8,128)(2,1)}, u32[]{:S(2)}, u32[]{:S(2)}) %all-to-all-start.5) | async-done | bytes 1048608 | tf_op jit(solution)/shard_map/all_to_all | solution.py:261
  875.2 17.3 %all-to-all-done.3 = bf16[8,128,512]{2,1,0:T(8,128)(2,1)S(1)} async-done(((bf16[8,128,512]{2,1,0:T(8,128)(2,1)}), bf16[8,128,512]{2,1,0:T(8,128)(2,1)S(1)}, u32[]{:S(2)}, u32[]{:S(2)}) %all-to-all-start.3) | async-done | bytes 1048608 | tf_op jit(solution)/shard_map/all_to_all | solution.py:260
  (577 shorter events, 534.9 us)
Async XLA Ops:
  3.6 33.2 %all-to-all-start = ((bf16[128,8,512]{2,0,1:T(8,128)(2,1)}), bf16[128,8,512]{2,0,1:T(8,128)(2,1)S(1)}, u32[]{:S(2)}, u32[]{:S(2)}) async-start(bf16[128,8,512]{2,0,1:T(8,128)(2,1)} %copy.54), calls=%async_computation | async-start | bytes 2097152 | tf_op jit(solution)/shard_map/all_to_all | solution.py:226
  12.1 28.3 %copy-start.45 = (bf16[128,4096]{1,0:T(8,128)(2,1)S(1)}, bf16[128,4096]{1,0:T(8,128)(2,1)}, u32[]{:S(2)}) copy-start(bf16[128,4096]{1,0:T(8,128)(2,1)} %param.24) | copy-start | bytes 3145732
  36.8 29.5 %all-to-all-start.1 = ((bf16[128,8,512]{2,0,1:T(8,128)(2,1)}), bf16[128,8,512]{2,0,1:T(8,128)(2,1)S(1)}, u32[]{:S(2)}, u32[]{:S(2)}) async-start(bf16[128,8,512]{2,0,1:T(8,128)(2,1)} %bitcast.315), calls=%async_computation.1 | async-start | bytes 2097152 | tf_op jit(solution)/shard_map/all_to_all | solution.py:227
  41.4 28.5 %copy-start.59 = (s32[32]{0:T(128)S(1)}, s32[32]{0:T(128)}, u32[]{:S(2)}) copy-start(s32[32]{0:T(128)} %param.27) | copy-start | bytes 388
  41.4 30.5 %copy-start.43 = (s32[32,16,12]{0,1,2:T(8,128)S(1)}, s32[32,16,12]{0,1,2:T(8,128)}, u32[]{:S(2)}) copy-start(s32[32,16,12]{0,1,2:T(8,128)} %param.26) | copy-start | bytes 73732
  66.3 29.6 %all-to-all-start.2 = ((bf16[128,8,512]{2,0,1:T(8,128)(2,1)}), bf16[128,8,512]{2,0,1:T(8,128)(2,1)S(1)}, u32[]{:S(2)}, u32[]{:S(2)}) async-start(bf16[128,8,512]{2,0,1:T(8,128)(2,1)} %bitcast.595), calls=%async_computation.2 | async-start | bytes 2097152 | tf_op jit(solution)/shard_map/all_to_all | solution.py:228
  95.9 55.3 %all-to-all-start.4 = ((bf16[128,8,512]{2,0,1:T(8,128)(2,1)}), bf16[128,8,512]{2,0,1:T(8,128)(2,1)}, u32[]{:S(2)}, u32[]{:S(2)}) async-start(bf16[128,8,512]{2,0,1:T(8,128)(2,1)} %copy.62), calls=%async_computation.4 | async-start | bytes 2097152 | tf_op jit(solution)/shard_map/all_to_all | solution.py:229
  344.3 108.1 %copy-start.2 = (bf16[16,64,128]{2,1,0:T(8,128)(2,1)S(1)}, bf16[16,64,128]{2,1,0:T(8,128)(2,1)}, u32[]{:S(2)}) copy-start(bf16[16,64,128]{2,1,0:T(8,128)(2,1)} %get-tuple-element.2385) | copy-start | bytes 786436
  344.3 108.1 %copy-start.3 = (bf16[16,64,128]{2,1,0:T(8,128)(2,1)S(1)}, bf16[16,64,128]{2,1,0:T(8,128)(2,1)}, u32[]{:S(2)}) copy-start(bf16[16,64,128]{2,1,0:T(8,128)(2,1)} %get-tuple-element.2389) | copy-start | bytes 786436
  344.3 108.2 %copy-start.57 = (s32[1,16,12]{2,1,0:T(8,128)S(1)}, s32[1,16,12]{2,1,0:T(8,128)}, u32[]{:S(2)}) copy-start(s32[1,16,12]{2,1,0:T(8,128)} %copy.58) | copy-start | bytes 2308
  452.4 50.9 %copy-start.21 = (bf16[16,64,128]{2,1,0:T(8,128)(2,1)S(1)}, bf16[16,64,128]{2,1,0:T(8,128)(2,1)}, u32[]{:S(2)}) copy-start(bf16[16,64,128]{2,1,0:T(8,128)(2,1)} %get-tuple-element.1450) | copy-start | bytes 786436
  503.4 108.0 %copy-start = (bf16[16,64,128]{2,1,0:T(8,128)(2,1)S(1)}, bf16[16,64,128]{2,1,0:T(8,128)(2,1)}, u32[]{:S(2)}) copy-start(bf16[16,64,128]{2,1,0:T(8,128)(2,1)} %get-tuple-element.2337) | copy-start | bytes 786436
  503.4 108.0 %copy-start.1 = (bf16[16,64,128]{2,1,0:T(8,128)(2,1)S(1)}, bf16[16,64,128]{2,1,0:T(8,128)(2,1)}, u32[]{:S(2)}) copy-start(bf16[16,64,128]{2,1,0:T(8,128)(2,1)} %get-tuple-element.2341) | copy-start | bytes 786436
  503.4 108.0 %copy-start.56 = (s32[1,16,12]{2,1,0:T(8,128)S(1)}, s32[1,16,12]{2,1,0:T(8,128)}, u32[]{:S(2)}) copy-start(s32[1,16,12]{2,1,0:T(8,128)} %copy.59) | copy-start | bytes 2308
  611.4 52.3 %copy-start.20 = (bf16[16,64,128]{2,1,0:T(8,128)(2,1)S(1)}, bf16[16,64,128]{2,1,0:T(8,128)(2,1)}, u32[]{:S(2)}) copy-start(bf16[16,64,128]{2,1,0:T(8,128)(2,1)} %get-tuple-element.1449) | copy-start | bytes 786436
  772.8 31.2 %all-to-all-start.7 = ((bf16[8,128,512]{2,1,0:T(8,128)(2,1)}), bf16[8,128,512]{2,1,0:T(8,128)(2,1)S(1)}, u32[]{:S(2)}, u32[]{:S(2)}) async-start(bf16[8,128,512]{2,1,0:T(8,128)(2,1)} %bitcast.596), calls=%async_computation.7 | async-start | bytes 2097152 | tf_op jit(solution)/shard_map/all_to_all | solution.py:271
  780.0 27.6 %copy-start.55 = (bf16[2,8,64,128]{3,2,1,0:T(8,128)(2,1)S(1)}, bf16[2,8,64,128]{3,2,1,0:T(8,128)(2,1)}, u32[]{:S(2)}) copy-start(bf16[2,8,64,128]{3,2,1,0:T(8,128)(2,1)} %get-tuple-element.1184) | copy-start | bytes 786436
  804.0 29.3 %all-to-all-start.6 = ((bf16[8,128,512]{2,1,0:T(8,128)(2,1)}), bf16[8,128,512]{2,1,0:T(8,128)(2,1)S(1)}, u32[]{:S(2)}, u32[]{:S(2)}) async-start(bf16[8,128,512]{2,1,0:T(8,128)(2,1)} %bitcast.130), calls=%async_computation.6 | async-start | bytes 2097152 | tf_op jit(solution)/shard_map/all_to_all | solution.py:268
  808.7 28.9 %copy-start.23 = (bf16[2,8,64,128]{3,2,1,0:T(8,128)(2,1)S(1)}, bf16[2,8,64,128]{3,2,1,0:T(8,128)(2,1)}, u32[]{:S(2)}) copy-start(bf16[2,8,64,128]{3,2,1,0:T(8,128)(2,1)} %get-tuple-element.2528) | copy-start | bytes 786436
  808.7 28.9 %copy-start.27 = (bf16[2,8,64,128]{3,2,1,0:T(8,128)(2,1)S(1)}, bf16[2,8,64,128]{3,2,1,0:T(8,128)(2,1)}, u32[]{:S(2)}) copy-start(bf16[2,8,64,128]{3,2,1,0:T(8,128)(2,1)} %get-tuple-element.2529) | copy-start | bytes 786436
  808.7 28.9 %copy-start.31 = (bf16[2,8,64,128]{3,2,1,0:T(8,128)(2,1)S(1)}, bf16[2,8,64,128]{3,2,1,0:T(8,128)(2,1)}, u32[]{:S(2)}) copy-start(bf16[2,8,64,128]{3,2,1,0:T(8,128)(2,1)} %get-tuple-element.2530) | copy-start | bytes 786436
  808.7 28.9 %copy-start.35 = (bf16[2,8,64,128]{3,2,1,0:T(8,128)(2,1)S(1)}, bf16[2,8,64,128]{3,2,1,0:T(8,128)(2,1)}, u32[]{:S(2)}) copy-start(bf16[2,8,64,128]{3,2,1,0:T(8,128)(2,1)} %get-tuple-element.2531) | copy-start | bytes 786436
  833.3 29.9 %all-to-all-start.5 = ((bf16[8,128,512]{2,1,0:T(8,128)(2,1)}), bf16[8,128,512]{2,1,0:T(8,128)(2,1)}, u32[]{:S(2)}, u32[]{:S(2)}) async-start(bf16[8,128,512]{2,1,0:T(8,128)(2,1)} %pad_maximum_fusion.1), calls=%async_computation.5 | async-start | bytes 2097152 | tf_op jit(solution)/shard_map/all_to_all | solution.py:261
  863.2 29.4 %all-to-all-start.3 = ((bf16[8,128,512]{2,1,0:T(8,128)(2,1)}), bf16[8,128,512]{2,1,0:T(8,128)(2,1)S(1)}, u32[]{:S(2)}, u32[]{:S(2)}) async-start(bf16[8,128,512]{2,1,0:T(8,128)(2,1)} %pad_maximum_fusion), calls=%async_computation.3 | async-start | bytes 2097152 | tf_op jit(solution)/shard_map/all_to_all | solution.py:260
  (78 other events, 291.9 us)
where the time goes:
time: 904 us; the launch traced here: 895 us
  matrix products  374 us (41%)
  other arithmetic  181 us (20%)
  waiting for transfers between devices  150 us (17%)
  local copies, waits for them, and re-layouts  116 us (13%)
  starting transfers between devices  36.1 us (4%)
  loops' own time  30.8 us (3%)
    dot_general x16, matrix products, group_scores(): jnp.einsum('gae,gke->gak', query_tile, keys_tile, preferred_element_type=...  284 us
    scatter-add x8, other arithmetic, one_group(): values_sum.at[flat_ids].add(values_part)  82.5 us
    scatter-add x8, other arithmetic, one_group(): keys_sum.at[flat_ids].add(keys_part)  82.5 us
    gather x16, local copies, waits for them, and re-layouts, one_group(): values_tile = value_rows[chosen].reshape(query_tile.shape[0], -1, head_size)  31.7 us
    another operation x4, loops' own time, head_backward(): lax.scan(one_group, (zeros_start, zeros_start), operands)  28.5 us
    all_to_all x1, waiting for transfers between devices, local(): lax.all_to_all(keys, 'seq', split_axis=1, concat_axis=0, tiled=True)  24.9 us
    all_to_all x1, waiting for transfers between devices, local(): lax.all_to_all(queries, 'seq', split_axis=1, concat_axis=0, tiled=True)  24.7 us
    all_to_all x1, waiting for transfers between devices, local(): lax.all_to_all(keys_grad.reshape(seq_len, width_local), 'seq', split_axis...  24.6 us
  transfers between devices with their start and end apart: 8, of which 7 were waited for; matrix products, arithmetic and copies ran while one was open for 8% of the time, Pallas kernels for 0%

commit v1 on v0

v1 whole, which is shorter than its diff:
```python
import functools
import math

import jax
import jax.numpy as jnp
from jax import lax
from jax.experimental import pallas as pl
from jax.experimental.pallas import tpu as pltpu
from jax.sharding import PartitionSpec as P

HEADS = 32
HEAD_DIM = 128
BLOCK = 64

very_low = -1e30
MESH = pl.DeviceIdType.MESH


def dot(a, b, dims):
    return lax.dot_general(a, b, (dims, ((), ())), preferred_element_type=jnp.float32)


LAST = ((1,), (1,))
PLAIN = ((1,), (0,))
FIRST = ((0,), (0,))


def build_masks(head, lists_ref, dilation_ref, row_codes, key_codes):
    blocks, slots = lists_ref.shape[1], lists_ref.shape[2]
    seq = row_codes.shape[1]
    spacing = dilation_ref[head].astype(jnp.float32)
    inverse = 1.0 / jnp.full((1, 128), spacing, jnp.float32)

    def residue(ids, inv):
        ids = ids.astype(jnp.float32)
        return ids - spacing * jnp.floor((ids + 0.5) * inv)

    lists = lists_ref[head]
    key_ids = lax.broadcasted_iota(jnp.int32, (blocks, blocks), 1)
    member = jnp.zeros((blocks, blocks), jnp.float32)
    for slot in range(slots):
        member = jnp.where(lists[:, slot : slot + 1] == key_ids, 1.0, member)
    spread = (
        lax.broadcasted_iota(jnp.int32, (blocks, seq), 1) // BLOCK
        == lax.broadcasted_iota(jnp.int32, (blocks, seq), 0)
    )
    listed = dot(member, spread.astype(jnp.float32), FIRST)
    query_ids = lax.broadcasted_iota(jnp.int32, (blocks, seq), 1)
    row_codes[...] = jnp.where(listed > 0.5, residue(query_ids, inverse[:, :1]), -1.0)
    key_codes[...] = residue(lax.broadcasted_iota(jnp.int32, (seq, 128), 0), inverse)


def attend_tile(start, reach, diagonal_only, tile, chunk, ins, outs, row_codes, key_codes, scratch):
    queries, keys, values, grads = ins
    attended, queries_grad = outs
    keys_t, values_t, keys_sum, values_sum = scratch
    scale = 1.0 / math.sqrt(HEAD_DIM)
    rows = pl.ds(start, tile)
    query, grad = queries[rows, :], grads[rows, :]
    chunks = reach // chunk
    query_ids = start + lax.broadcasted_iota(jnp.int32, (chunk, tile), 1)
    scores = []
    for c in range(chunks):
        span = slice(c * chunk, (c + 1) * chunk)
        raw = dot(keys[span, :], query, LAST)
        codes = key_codes[span, :]
        codes = jnp.concatenate([codes] * (tile // 128), axis=1) if tile > 128 else codes
        first = c * chunk // BLOCK
        wanted = jnp.concatenate(
            [
                jnp.broadcast_to(row_codes[first + b : first + b + 1, rows], (BLOCK, tile))
                for b in range(chunk // BLOCK)
            ],
            axis=0,
        )
        seen = codes == wanted
        if not diagonal_only or c == chunks - 1:
            key_ids = c * chunk + lax.broadcasted_iota(jnp.int32, (chunk, tile), 0)
            seen = seen & (key_ids <= query_ids)
        scores.append(jnp.where(seen, raw, very_low / scale))
    top = functools.reduce(jnp.maximum, [jnp.max(s, axis=0, keepdims=True) for s in scores])
    expos = [jnp.exp2((s - top) * (scale * math.log2(math.e))) for s in scores]
    total = sum(jnp.sum(e, axis=0, keepdims=True) for e in expos)
    share = 1.0 / total
    weights = [e * share for e in expos]
    weights16 = [w.astype(jnp.bfloat16) for w in weights]
    out_t = sum(
        dot(values_t[:, c * chunk : (c + 1) * chunk], weights16[c], PLAIN) for c in range(chunks)
    )
    out16 = jnp.transpose(out_t).astype(jnp.bfloat16)
    attended[rows, :] = out16
    product_t = jnp.transpose(grad.astype(jnp.float32) * out16.astype(jnp.float32))
    delta = jnp.sum(product_t, axis=0, keepdims=True)
    query_t = None
    for c in range(chunks):
        span = slice(c * chunk, (c + 1) * chunk)
        values_sum[span, :] += dot(weights16[c], grad, PLAIN)
        dweights = dot(values[span, :], grad, LAST)
        dscores16 = (weights[c] * (dweights - delta)).astype(jnp.bfloat16)
        keys_sum[span, :] += dot(dscores16, query, PLAIN)
        part = dot(keys_t[:, span], dscores16, PLAIN)
        query_t = part if query_t is None else query_t + part
    queries_grad[rows, :] = jnp.transpose(query_t * scale).astype(jnp.bfloat16)


def attend_head(ins, outs, row_codes, key_codes, scratch):
    keys_t, values_t, keys_sum, values_sum = scratch
    _, keys, values, _ = ins
    attended, queries_grad, keys_grad, values_grad = outs
    seq = keys.shape[0]
    keys_t[...] = jnp.transpose(keys[...].astype(jnp.float32)).astype(jnp.bfloat16)
    values_t[...] = jnp.transpose(values[...].astype(jnp.float32)).astype(jnp.bfloat16)
    keys_sum[...] = jnp.zeros_like(keys_sum)
    values_sum[...] = jnp.zeros_like(values_sum)
    tile_outs = (attended, queries_grad)
    if seq <= 1024:
        for index in range(seq // 256):
            attend_tile(
                index * 256, (index + 1) * 256, True, 256, 256, ins, tile_outs, row_codes, key_codes, scratch
            )
    else:

        def one(index, carry):
            start = pl.multiple_of(index * 128, 128)
            attend_tile(start, seq, False, 128, 256, ins, tile_outs, row_codes, key_codes, scratch)
            return carry

        lax.fori_loop(0, seq // 128, one, 0)
    keys_grad[...] = (keys_sum[...] * (1.0 / math.sqrt(HEAD_DIM))).astype(jnp.bfloat16)
    values_grad[...] = values_sum[...].astype(jnp.bfloat16)


def kernel(
    n,
    heads,
    queries,
    keys,
    values,
    grads,
    lists_ref,
    dilation_ref,
    attended,
    queries_grad,
    keys_grad,
    values_grad,
    held,
    made,
    row_codes,
    key_codes,
    keys_t,
    values_t,
    keys_sum,
    values_sum,
    in_send,
    in_recv,
    out_send,
    out_recv,
):
    me = lax.axis_index("seq")
    tokens = queries.shape[0]
    sources = (queries, keys, values, grads)
    targets = (attended, queries_grad, keys_grad, values_grad)
    my_rows = pl.ds(pl.multiple_of(me * tokens, tokens), tokens)

    def columns(owner, head):
        return pl.ds(pl.multiple_of((owner * heads + head) * HEAD_DIM, HEAD_DIM), HEAD_DIM)

    barrier = pltpu.get_barrier_semaphore()

    def greet(step, carry):
        pl.semaphore_signal(
            barrier, inc=1, device_id={"seq": lax.rem(me + step, n)}, device_id_type=MESH
        )
        return carry

    lax.fori_loop(1, n, greet, 0)
    pl.semaphore_wait(barrier, n - 1)

    def send_head(head, carry):
        def send_one(step, inner):
            other = lax.rem(me + step, n)
            for index, source in enumerate(sources):
                pltpu.make_async_remote_copy(
                    src_ref=source.at[:, columns(other, head)],
                    dst_ref=held.at[head, index, my_rows, :],
                    send_sem=in_send.at[head],
                    recv_sem=in_recv.at[head],
                    device_id={"seq": other},
                    device_id_type=MESH,
                ).start()
            return inner

        for index, source in enumerate(sources):
            pltpu.make_async_copy(
                source.at[:, columns(me, head)], held.at[head, index, my_rows, :], in_recv.at[head]
            ).start()
        lax.fori_loop(1, n, send_one, 0)
        return carry

    lax.fori_loop(0, heads, send_head, 0)

    def work_head(head, carry):
        build_masks(me * heads + head, lists_ref, dilation_ref, row_codes, key_codes)
        pltpu.make_async_copy(held.at[head], held.at[head], in_recv.at[head]).wait()
        attend_head(
            tuple(held.at[head, index] for index in range(4)),
            tuple(made.at[head, index] for index in range(4)),
            row_codes,
            key_codes,
            (keys_t, values_t, keys_sum, values_sum),
        )

        def send_one(step, inner):
            other = lax.rem(me + step, n)
            rows = pl.ds(pl.multiple_of(other * tokens, tokens), tokens)
            for index, target in enumerate(targets):
                pltpu.make_async_remote_copy(
                    src_ref=made.at[head, index, rows, :],
                    dst_ref=target.at[:, columns(me, head)],
                    send_sem=out_send.at[head],
                    recv_sem=out_recv.at[index],
                    device_id={"seq": other},
                    device_id_type=MESH,
                ).start()
            return inner

        for index, target in enumerate(targets):
            pltpu.make_async_copy(
                made.at[head, index, my_rows, :], target.at[:, columns(me, head)], out_recv.at[index]
            ).start()
        lax.fori_loop(1, n, send_one, 0)
        return carry

    lax.fori_loop(0, heads, work_head, 0)

    sent = (n - 1) * tokens

    def finish(head, carry):
        part = held.at[head, :, pl.ds(0, sent), :]
        pltpu.make_async_copy(part, part, in_send.at[head]).wait()
        part = made.at[head, :, pl.ds(0, sent), :]
        pltpu.make_async_copy(part, part, out_send.at[head]).wait()
        return carry

    lax.fori_loop(0, heads, finish, 0)
    for index, target in enumerate(targets):
        pltpu.make_async_copy(target, target, out_recv.at[index]).wait()


def local(queries, keys, values, out_grad, key_blocks, dilation):
    n = lax.axis_size("seq")
    heads = HEADS // n
    tokens, width = queries.shape
    seq = tokens * n
    blocks = key_blocks.shape[1]
    row = jax.ShapeDtypeStruct((tokens, width), jnp.bfloat16)
    anywhere = pl.BlockSpec(memory_space=pl.ANY)
    return pl.pallas_call(
        functools.partial(kernel, n, heads),
        out_shape=(row,) * 4,
        in_specs=[anywhere] * 4
        + [pl.BlockSpec(memory_space=pltpu.VMEM), pl.BlockSpec(memory_space=pltpu.SMEM)],
        out_specs=(anywhere,) * 4,
        scratch_shapes=[
            pltpu.VMEM((heads, 4, seq, HEAD_DIM), jnp.bfloat16),
            pltpu.VMEM((heads, 4, seq, HEAD_DIM), jnp.bfloat16),
            pltpu.VMEM((blocks, seq), jnp.float32),
            pltpu.VMEM((seq, 128), jnp.float32),
            pltpu.VMEM((HEAD_DIM, seq), jnp.bfloat16),
            pltpu.VMEM((HEAD_DIM, seq), jnp.bfloat16),
            pltpu.VMEM((seq, HEAD_DIM), jnp.float32),
            pltpu.VMEM((seq, HEAD_DIM), jnp.float32),
            pltpu.SemaphoreType.DMA((heads,)),
            pltpu.SemaphoreType.DMA((heads,)),
            pltpu.SemaphoreType.DMA((heads,)),
            pltpu.SemaphoreType.DMA((4,)),
        ],
        compiler_params=pltpu.CompilerParams(
            collective_id=0, has_side_effects=True, vmem_limit_bytes=48 * 1024 * 1024
        ),
    )(queries, keys, values, out_grad, key_blocks, dilation)


def solution(mesh):
    rows = P(("batch", "seq"), None)
    return jax.shard_map(
        local,
        mesh=mesh,
        in_specs=(rows, rows, rows, rows, P("batch", None, None), P("batch")),
        out_specs=(rows, rows, rows, rows),
        check_vma=False,
    )
```

time: 904 us -> 192 us (0.21)
  the two profiles are of different devices: /device:TPU:0 before, /device:TPU:13 now
where the time goes in v1:
time: 192 us
  Pallas kernels  185 us (96%)
  local copies, waits for them, and re-layouts  6.2 us (3%)
    pallas_call x1, Pallas kernels, local(): pl.pallas_call(functools.partial(kernel, n, heads), out_shape=(row,) * 4,...  185 us
    unnamed x9, local copies, waits for them, and re-layouts  6.2 us

profile of v1, /device:TPU:13, one launch (start us, length us, event | category | flops | bytes accessed | tf_op | source)
XLA Modules:
  0.0 192.3 jit_solution(15751340177540721743)
XLA Ops:
  0.6 0.0 copy-start.1
  0.6 1.1 copy.10.lists_ref
  1.7 0.0 copy-done.1
  1.8 0.0 copy-start
  1.8 1.2 copy-done
  3.0 185.4 %shard_map.93 = (bf16[128,4096]{1,0:T(8,128)(2,1)S(1)}, bf16[128,4096]{1,0:T(8,128)(2,1)S(1)}, bf16[128,4096]{1,0:T(8,128)(2,1)S(1)}, bf16[128,4096]{1,0:T(8,128)(2,1)S(1)}) custom-call(bf16[128,4096]{1,0:T(8,128)(2,1)S(1)} %copy-done, bf16[128,4096]{1,0:T(8,128)(2,1)} %keys.1, bf16[128,4096]{1,0:T(8,128)(2,1)} %values.1, bf16[128,4096]{1,0:T(8,128)(2,1)} %grads.1, ...), custom_call_target="tpu_custom_call" | custom-call | tf_op jit(solution)/shard_map/pallas_call | solution.py:258
  188.4 1.0 copy.15
  189.4 1.0 copy.16
  190.4 1.0 copy.17
  191.3 1.0 copy.18
Async XLA Ops:
  0.6 1.1 copy-start.1
  1.8 1.2 copy-start

commit v2 on v1

--- a/solution.py
+++ b/solution.py
@@ -50,19 +50,19 @@
     key_codes[...] = residue(lax.broadcasted_iota(jnp.int32, (seq, 128), 0), inverse)
 
 
-def attend_tile(start, reach, diagonal_only, tile, chunk, ins, outs, row_codes, key_codes, scratch):
-    queries, keys, values, grads = ins
-    attended, queries_grad = outs
+def attend_tile(
+    start, chunks, diagonal_only, query, grad, key_at, value_at, attended, queries_grad, row_codes, key_codes, scratch
+):
     keys_t, values_t, keys_sum, values_sum = scratch
     scale = 1.0 / math.sqrt(HEAD_DIM)
+    tile = query.shape[0]
     rows = pl.ds(start, tile)
-    query, grad = queries[rows, :], grads[rows, :]
-    chunks = reach // chunk
+    chunk = 256
     query_ids = start + lax.broadcasted_iota(jnp.int32, (chunk, tile), 1)
     scores = []
     for c in range(chunks):
         span = slice(c * chunk, (c + 1) * chunk)
-        raw = dot(keys[span, :], query, LAST)
+        raw = dot(key_at(c), query, LAST)
         codes = key_codes[span, :]
         codes = jnp.concatenate([codes] * (tile // 128), axis=1) if tile > 128 else codes
         first = c * chunk // BLOCK
@@ -88,46 +88,330 @@
         dot(values_t[:, c * chunk : (c + 1) * chunk], weights16[c], PLAIN) for c in range(chunks)
     )
     out16 = jnp.transpose(out_t).astype(jnp.bfloat16)
-    attended[rows, :] = out16
+    attended[...] = out16
     product_t = jnp.transpose(grad.astype(jnp.float32) * out16.astype(jnp.float32))
     delta = jnp.sum(product_t, axis=0, keepdims=True)
     query_t = None
     for c in range(chunks):
         span = slice(c * chunk, (c + 1) * chunk)
         values_sum[span, :] += dot(weights16[c], grad, PLAIN)
-        dweights = dot(values[span, :], grad, LAST)
+        dweights = dot(value_at(c), grad, LAST)
         dscores16 = (weights[c] * (dweights - delta)).astype(jnp.bfloat16)
         keys_sum[span, :] += dot(dscores16, query, PLAIN)
         part = dot(keys_t[:, span], dscores16, PLAIN)
         query_t = part if query_t is None else query_t + part
-    queries_grad[rows, :] = jnp.transpose(query_t * scale).astype(jnp.bfloat16)
+    queries_grad[...] = jnp.transpose(query_t * scale).astype(jnp.bfloat16)
+
+
+def turned(rows):
+    return jnp.transpose(rows.astype(jnp.float32)).astype(jnp.bfloat16)
 
 
 def attend_head(ins, outs, row_codes, key_codes, scratch):
     keys_t, values_t, keys_sum, values_sum = scratch
-    _, keys, values, _ = ins
+    queries, keys, values, grads = ins
     attended, queries_grad, keys_grad, values_grad = outs
     seq = keys.shape[0]
-    keys_t[...] = jnp.transpose(keys[...].astype(jnp.float32)).astype(jnp.bfloat16)
-    values_t[...] = jnp.transpose(values[...].astype(jnp.float32)).astype(jnp.bfloat16)
+    keys_t[...] = turned(keys[...])
+    values_t[...] = turned(values[...])
     keys_sum[...] = jnp.zeros_like(keys_sum)
     values_sum[...] = jnp.zeros_like(values_sum)
-    tile_outs = (attended, queries_grad)
-    if seq <= 1024:
-        for index in range(seq // 256):
-            attend_tile(
-                index * 256, (index + 1) * 256, True, 256, 256, ins, tile_outs, row_codes, key_codes, scratch
-            )
-    else:
-
-        def one(index, carry):
-            start = pl.multiple_of(index * 128, 128)
-            attend_tile(start, seq, False, 128, 256, ins, tile_outs, row_codes, key_codes, scratch)
-            return carry
-
-        lax.fori_loop(0, seq // 128, one, 0)
+
+    def one(index, carry):
+        start = pl.multiple_of(index * 128, 128)
+        rows = pl.ds(start, 128)
+        attend_tile(
+            start,
+            seq // 256,
+            False,
+            queries[rows, :],
+            grads[rows, :],
+            lambda c: keys[c * 256 : (c + 1) * 256, :],
+            lambda c: values[c * 256 : (c + 1) * 256, :],
+            attended.at[rows, :],
+            queries_grad.at[rows, :],
+            row_codes,
+            key_codes,
+            scratch,
+        )
+        return carry
+
+    lax.fori_loop(0, seq // 128, one, 0)
     keys_grad[...] = (keys_sum[...] * (1.0 / math.sqrt(HEAD_DIM))).astype(jnp.bfloat16)
     values_grad[...] = values_sum[...].astype(jnp.bfloat16)
+
+
+def attend_half(upper, held, low, made, row_codes, key_codes, scratch):
+    keys_t, values_t, keys_sum, values_sum = scratch
+    half = held.shape[1]
+    before = half if upper else 0
+    reach = before + half
+
+    def rows_at(index, c):
+        if c * 256 < before:
+            return low[index - 1, c * 256 : (c + 1) * 256, :]
+        return held[index, c * 256 - before : (c + 1) * 256 - before, :]
+
+    for c in range(reach // 256):
+        span = slice(c * 256, (c + 1) * 256)
+        keys_t[:, span] = turned(rows_at(1, c))
+        values_t[:, span] = turned(rows_at(2, c))
+    keys_sum[:reach, :] = jnp.zeros((reach, HEAD_DIM), jnp.float32)
+    values_sum[:reach, :] = jnp.zeros((reach, HEAD_DIM), jnp.float32)
+    for tile in range(half // 256):
+        rows = slice(tile * 256, (tile + 1) * 256)
+        start = before + tile * 256
+        attend_tile(
+            start,
+            start // 256 + 1,
+            True,
+            held[0, rows, :],
+            held[3, rows, :],
+            functools.partial(rows_at, 1),
+            functools.partial(rows_at, 2),
+            made.at[0, rows, :],
+            made.at[1, rows, :],
+            row_codes,
+            key_codes,
+            scratch,
+        )
+
+
+def split_kernel(
+    lag,
+    relay_lag,
+    queries,
+    keys,
+    values,
+    grads,
+    lists_ref,
+    dilation_ref,
+    attended,
+    queries_grad,
+    keys_grad,
+    values_grad,
+    held,
+    made,
+    low_in,
+    low_out,
+    stage_in,
+    stage_out,
+    sums,
+    row_codes,
+    key_codes,
+    keys_t,
+    values_t,
+    keys_sum,
+    values_sum,
+    held_recv,
+    low_recv,
+    stage_in_recv,
+    stage_out_recv,
+    out_recv,
+    send,
+    low_send,
+):
+    me = lax.axis_index("seq")
+    tokens = queries.shape[0]
+    heads = HEADS // 2
+    half = 4 * tokens
+    side = lax.rem(me, 2)
+    plane = me // 2
+    across = me + 1 - 2 * side
+    along = me + 2 - 4 * lax.rem(plane, 2)
+    middle = 6 - 2 * plane + side
+    inner = (plane == 1) | (plane == 2)
+    sources = (queries, keys, values, grads)
+    targets = (attended, queries_grad, keys_grad, values_grad)
+    scale = 1.0 / math.sqrt(HEAD_DIM)
+    scratch = (keys_t, values_t, keys_sum, values_sum)
+
+    def columns(which, head):
+        return pl.ds(pl.multiple_of((which * heads + head) * HEAD_DIM, HEAD_DIM), HEAD_DIM)
+
+    def rows_of(device):
+        return pl.ds(pl.multiple_of(lax.rem(device, 4) * tokens, tokens), tokens)
+
+    def push(src, dst, send_sem, recv_sem, device):
+        pltpu.make_async_remote_copy(
+            src_ref=src,
+            dst_ref=dst,
+            send_sem=send_sem,
+            recv_sem=recv_sem,
+            device_id={"seq": device},
+            device_id_type=MESH,
+        ).start()
+
+    def wait_for(ref, sem):
+        pltpu.make_async_copy(ref, ref, sem).wait()
+
+    def loop(count, body):
+        def step(k, carry):
+            body(k)
+            return carry
+
+        lax.fori_loop(0, count, step, 0)
+
+    barrier = pltpu.get_barrier_semaphore()
+
+    def greet(device):
+        pl.semaphore_signal(barrier, inc=1, device_id={"seq": device}, device_id_type=MESH)
+
+    def outer_role():
+        greet(across)
+        greet(along)
+        pl.semaphore_wait(barrier, 2)
+
+        def exchange(k):
+            for index, source in enumerate(sources):
+                push(
+                    source.at[:, columns(1 - side, k)],
+                    stage_in.at[k, index],
+                    send.at[0],
+                    stage_in_recv.at[k],
+                    across,
+                )
+
+        loop(heads, exchange)
+
+        def relay_out(k):
+            wait_for(stage_out.at[k], stage_out_recv.at[k])
+            for index, target in enumerate(targets):
+                push(
+                    stage_out.at[k, index],
+                    target.at[:, columns(side, k)],
+                    send.at[0],
+                    out_recv.at[index],
+                    across,
+                )
+
+        def relay_in(k):
+            for index, source in enumerate(sources):
+                push(
+                    source.at[:, columns(side, k)],
+                    held.at[k, index, rows_of(me), :],
+                    send.at[0],
+                    held_recv.at[k],
+                    along,
+                )
+            wait_for(stage_in.at[k], stage_in_recv.at[k])
+            for index in range(4):
+                push(
+                    stage_in.at[k, index],
+                    held.at[k, index, rows_of(across), :],
+                    send.at[0],
+                    held_recv.at[k],
+                    along,
+                )
+
+        def both(k):
+            relay_in(k)
+
+            @pl.when(k >= relay_lag)
+            def _():
+                relay_out(k - relay_lag)
+
+        loop(heads, both)
+        loop(relay_lag, lambda k: relay_out(heads - relay_lag + k))
+
+    def give(index, k):
+        target = targets[index]
+        far = rows_of(along + across - me)
+        pltpu.make_async_copy(
+            made.at[k, index, rows_of(me), :], target.at[:, columns(side, k)], out_recv.at[index]
+        ).start()
+        push(made.at[k, index, far, :], stage_out.at[k, index], send.at[0], stage_out_recv.at[k], along)
+        push(
+            made.at[k, index, rows_of(along), :],
+            target.at[:, columns(side, k)],
+            send.at[0],
+            out_recv.at[index],
+            along,
+        )
+        push(
+            made.at[k, index, rows_of(across), :],
+            target.at[:, columns(side, k)],
+            send.at[0],
+            out_recv.at[index],
+            across,
+        )
+
+    def inner_start():
+        greet(across)
+        greet(along)
+        greet(middle)
+        pl.semaphore_wait(barrier, 3)
+
+        def exchange(k):
+            for index, source in enumerate(sources):
+                pltpu.make_async_copy(
+                    source.at[:, columns(side, k)],
+                    held.at[k, index, rows_of(me), :],
+                    held_recv.at[k],
+                ).start()
+                push(
+                    source.at[:, columns(1 - side, k)],
+                    held.at[k, index, rows_of(me), :],
+                    send.at[0],
+                    held_recv.at[k],
+                    across,
+                )
+
+        loop(heads, exchange)
+
+    def lower_role():
+        inner_start()
+
+        def finish(k):
+            wait_for(low_in.at[k], low_recv.at[k])
+            made[k, 2] = ((sums[k, 0] + low_in[k, 0].astype(jnp.float32)) * scale).astype(jnp.bfloat16)
+            made[k, 3] = (sums[k, 1] + low_in[k, 1].astype(jnp.float32)).astype(jnp.bfloat16)
+            give(2, k)
+            give(3, k)
+
+        def step(k):
+            build_masks(side * heads + k, lists_ref, dilation_ref, row_codes, key_codes)
+            wait_for(held.at[k], held_recv.at[k])
+            push(held.at[k, pl.ds(1, 2)], low_in.at[k], low_send.at[0], low_recv.at[k], middle)
+            attend_half(False, held.at[k], None, made.at[k], row_codes, key_codes, scratch)
+            give(0, k)
+            give(1, k)
+            sums[k, 0] = keys_sum[:half, :]
+            sums[k, 1] = values_sum[:half, :]
+
+            @pl.when(k >= lag)
+            def _():
+                finish(k - lag)
+
+        loop(heads, step)
+        loop(lag, lambda k: finish(heads - lag + k))
+
+    def upper_role():
+        inner_start()
+
+        def step(k):
+            build_masks(side * heads + k, lists_ref, dilation_ref, row_codes, key_codes)
+            wait_for(held.at[k], held_recv.at[k])
+            wait_for(low_in.at[k], low_recv.at[k])
+            attend_half(True, held.at[k], low_in.at[k], made.at[k], row_codes, key_codes, scratch)
+            low_out[k, 0] = keys_sum[:half, :].astype(jnp.bfloat16)
+            low_out[k, 1] = values_sum[:half, :].astype(jnp.bfloat16)
+            push(low_out.at[k], low_in.at[k], low_send.at[0], low_recv.at[k], middle)
+            made[k, 2] = (keys_sum[half:, :] * scale).astype(jnp.bfloat16)
+            made[k, 3] = values_sum[half:, :].astype(jnp.bfloat16)
+            for index in range(4):
+                give(index, k)
+
+        loop(heads, step)
+
+    pl.when(jnp.logical_not(inner))(outer_role)
+    pl.when(plane == 1)(lower_role)
+    pl.when(plane == 2)(upper_role)
+
+    wait_for(held, send.at[0])
+    pl.when(inner)(lambda: wait_for(low_in, low_send.at[0]))
+    for index, target in enumerate(targets):
+        wait_for(target, out_recv.at[index])
 
 
 def kernel(
@@ -249,34 +533,61 @@
 
 def local(queries, keys, values, out_grad, key_blocks, dilation):
     n = lax.axis_size("seq")
-    heads = HEADS // n
     tokens, width = queries.shape
     seq = tokens * n
     blocks = key_blocks.shape[1]
     row = jax.ShapeDtypeStruct((tokens, width), jnp.bfloat16)
     anywhere = pl.BlockSpec(memory_space=pl.ANY)
+    work = [
+        pltpu.VMEM((blocks, seq), jnp.float32),
+        pltpu.VMEM((seq, 128), jnp.float32),
+        pltpu.VMEM((HEAD_DIM, seq), jnp.bfloat16),
+        pltpu.VMEM((HEAD_DIM, seq), jnp.bfloat16),
+        pltpu.VMEM((seq, HEAD_DIM), jnp.float32),
+        pltpu.VMEM((seq, HEAD_DIM), jnp.float32),
+    ]
+    if n == 8 and tokens % 64 == 0:
+        heads = HEADS // 2
+        half = seq // 2
+        body = functools.partial(split_kernel, 5, 8)
+        scratch = [
+            pltpu.VMEM((heads, 4, half, HEAD_DIM), jnp.bfloat16),
+            pltpu.VMEM((heads, 4, half, HEAD_DIM), jnp.bfloat16),
+            pltpu.VMEM((heads, 2, half, HEAD_DIM), jnp.bfloat16),
+            pltpu.VMEM((heads, 2, half, HEAD_DIM), jnp.bfloat16),
+            pltpu.VMEM((heads, 4, tokens, HEAD_DIM), jnp.bfloat16),
+            pltpu.VMEM((heads, 4, tokens, HEAD_DIM), jnp.bfloat16),
+            pltpu.VMEM((heads, 2, half, HEAD_DIM), jnp.float32),
+            *work,
+            pltpu.SemaphoreType.DMA((heads,)),
+            pltpu.SemaphoreType.DMA((heads,)),
+            pltpu.SemaphoreType.DMA((heads,)),
+            pltpu.SemaphoreType.DMA((heads,)),
+            pltpu.SemaphoreType.DMA((4,)),
+            pltpu.SemaphoreType.DMA((1,)),
+            pltpu.SemaphoreType.DMA((1,)),
+        ]
+    else:
+        heads = HEADS // n
+        body = functools.partial(kernel, n, heads)
+        scratch = [
+            pltpu.VMEM((heads, 4, seq, HEAD_DIM), jnp.bfloat16),
+            pltpu.VMEM((heads, 4, seq, HEAD_DIM), jnp.bfloat16),
+            *work,
+            pltpu.SemaphoreType.DMA((heads,)),
+            pltpu.SemaphoreType.DMA((heads,)),
+            pltpu.SemaphoreType.DMA((heads,)),
+            pltpu.SemaphoreType.DMA((4,)),
+        ]
     return pl.pallas_call(
-        functools.partial(kernel, n, heads),
+        body,
         out_shape=(row,) * 4,
         in_specs=[anywhere] * 4
         + [pl.BlockSpec(memory_space=pltpu.VMEM), pl.BlockSpec(memory_space=pltpu.SMEM)],
         out_specs=(anywhere,) * 4,
-        scratch_shapes=[
-            pltpu.VMEM((heads, 4, seq, HEAD_DIM), jnp.bfloat16),
-            pltpu.VMEM((heads, 4, seq, HEAD_DIM), jnp.bfloat16),
-            pltpu.VMEM((blocks, seq), jnp.float32),
-            pltpu.VMEM((seq, 128), jnp.float32),
-            pltpu.VMEM((HEAD_DIM, seq), jnp.bfloat16),
-            pltpu.VMEM((HEAD_DIM, seq), jnp.bfloat16),
-            pltpu.VMEM((seq, HEAD_DIM), jnp.float32),
-            pltpu.VMEM((seq, HEAD_DIM), jnp.float32),
-            pltpu.SemaphoreType.DMA((heads,)),
-            pltpu.SemaphoreType.DMA((heads,)),
-            pltpu.SemaphoreType.DMA((heads,)),
-            pltpu.SemaphoreType.DMA((4,)),
-        ],
+        scratch_shapes=scratch,
         compiler_params=pltpu.CompilerParams(
-            collective_id=0, has_side_effects=True, vmem_limit_bytes=48 * 1024 * 1024
+            collective_id=0, has_side_effects=True, vmem_limit_bytes=56 * 1024 * 1024
         ),
     )(queries, keys, values, out_grad, key_blocks, dilation)
 

time: 192 us -> 134 us (0.70)
  the two profiles are of different devices: /device:TPU:13 before, /device:TPU:0 now
where the time goes in v2:
time: 134 us; the launch traced here: 133 us
  Pallas kernels  124 us (93%)
  local copies, waits for them, and re-layouts  8.33 us (6%)
    pallas_call x1, Pallas kernels, local(): pl.pallas_call(body, out_shape=(row,) * 4, in_specs=[anywhere] * 4 + [pl....  124 us
    unnamed x11, local copies, waits for them, and re-layouts  8.33 us

profile of v2, /device:TPU:0, one launch (start us, length us, event | category | flops | bytes accessed | tf_op | source)
XLA Modules:
  0.0 133.4 jit_solution(4792324743017593612)
XLA Ops:
  0.6 1.8 %copy.10.lists_ref = s32[32,16,12]{2,1,0:T(8,128)} copy(s32[32,16,12]{0,1,2:T(8,128)} %param.10) | data formatting | bytes 49152 | tf_op args[4]
  2.4 124.4 %shard_map.93 = (bf16[128,4096]{1,0:T(8,128)(2,1)}, bf16[128,4096]{1,0:T(8,128)(2,1)}, bf16[128,4096]{1,0:T(8,128)(2,1)}, bf16[128,4096]{1,0:T(8,128)(2,1)}) custom-call(bf16[128,4096]{1,0:T(8,128)(2,1)} %queries.1, bf16[128,4096]{1,0:T(8,128)(2,1)} %keys.1, bf16[128,4096]{1,0:T(8,128)(2,1)} %values.1, bf16[128,4096]{1,0:T(8,128)(2,1)} %grads.1, ...), custom_call_target="tpu_custom_call" | custom-call | tf_op jit(solution)/shard_map/pallas_call | solution.py:582
  126.8 0.0 copy-start.2
  126.8 2.4 %copy.15 = bf16[128,4096]{1,0:T(8,128)(2,1)} copy(bf16[128,4096]{1,0:T(8,128)(2,1)} %get-tuple-element.8) | data formatting | bytes 2097152
  129.2 0.0 copy-done.2
  129.2 0.0 copy-start.1
  129.2 1.0 copy.16
  130.2 0.6 copy-done.1
  130.8 0.0 copy-start
  130.8 1.0 copy.17
  131.8 0.6 copy-done
  132.4 1.0 copy.18
Async XLA Ops:
  126.8 2.4 %copy-start.2 = (bf16[128,4096]{1,0:T(8,128)(2,1)S(1)}, bf16[128,4096]{1,0:T(8,128)(2,1)}, u32[]{:S(2)}) copy-start(bf16[128,4096]{1,0:T(8,128)(2,1)} %get-tuple-element.9) | copy-start | bytes 3145732
  129.2 1.6 %copy-start.1 = (bf16[128,4096]{1,0:T(8,128)(2,1)S(1)}, bf16[128,4096]{1,0:T(8,128)(2,1)}, u32[]{:S(2)}) copy-start(bf16[128,4096]{1,0:T(8,128)(2,1)} %get-tuple-element.10) | copy-start | bytes 3145732
  130.8 1.6 %copy-start = (bf16[128,4096]{1,0:T(8,128)(2,1)S(1)}, bf16[128,4096]{1,0:T(8,128)(2,1)}, u32[]{:S(2)}) copy-start(bf16[128,4096]{1,0:T(8,128)(2,1)} %get-tuple-element.11) | copy-start | bytes 3145732

commit v3 on v2

--- a/solution.py
+++ b/solution.py
@@ -26,7 +26,7 @@
 
 
 def build_masks(head, lists_ref, dilation_ref, row_codes, key_codes):
-    blocks, slots = lists_ref.shape[1], lists_ref.shape[2]
+    slots, blocks, count = lists_ref.shape
     seq = row_codes.shape[1]
     spacing = dilation_ref[head].astype(jnp.float32)
     inverse = 1.0 / jnp.full((1, 128), spacing, jnp.float32)
@@ -35,11 +35,12 @@
         ids = ids.astype(jnp.float32)
         return ids - spacing * jnp.floor((ids + 0.5) * inv)
 
-    lists = lists_ref[head]
+    mine = lax.broadcasted_iota(jnp.int32, (blocks, count), 1) == head
     key_ids = lax.broadcasted_iota(jnp.int32, (blocks, blocks), 1)
     member = jnp.zeros((blocks, blocks), jnp.float32)
     for slot in range(slots):
-        member = jnp.where(lists[:, slot : slot + 1] == key_ids, 1.0, member)
+        listed = jnp.sum(jnp.where(mine, lists_ref[slot], 0), axis=1, keepdims=True)
+        member = jnp.where(listed == key_ids, 1.0, member)
     spread = (
         lax.broadcasted_iota(jnp.int32, (blocks, seq), 1) // BLOCK
         == lax.broadcasted_iota(jnp.int32, (blocks, seq), 0)
@@ -141,34 +142,29 @@
     values_grad[...] = values_sum[...].astype(jnp.bfloat16)
 
 
-def attend_half(upper, held, low, made, row_codes, key_codes, scratch):
+def attend_rows(key_chunks, query_tiles, held, made, row_codes, key_codes, scratch):
     keys_t, values_t, keys_sum, values_sum = scratch
-    half = held.shape[1]
-    before = half if upper else 0
-    reach = before + half
 
     def rows_at(index, c):
-        if c * 256 < before:
-            return low[index - 1, c * 256 : (c + 1) * 256, :]
-        return held[index, c * 256 - before : (c + 1) * 256 - before, :]
-
-    for c in range(reach // 256):
+        ref, first = key_chunks[c]
+        return ref[index, first : first + 256, :]
+
+    for c in range(len(key_chunks)):
         span = slice(c * 256, (c + 1) * 256)
-        keys_t[:, span] = turned(rows_at(1, c))
-        values_t[:, span] = turned(rows_at(2, c))
-    keys_sum[:reach, :] = jnp.zeros((reach, HEAD_DIM), jnp.float32)
-    values_sum[:reach, :] = jnp.zeros((reach, HEAD_DIM), jnp.float32)
-    for tile in range(half // 256):
-        rows = slice(tile * 256, (tile + 1) * 256)
-        start = before + tile * 256
+        keys_t[:, span] = turned(rows_at(0, c))
+        values_t[:, span] = turned(rows_at(1, c))
+        keys_sum[span, :] = jnp.zeros((256, HEAD_DIM), jnp.float32)
+        values_sum[span, :] = jnp.zeros((256, HEAD_DIM), jnp.float32)
+    for first, start in query_tiles:
+        rows = slice(first, first + 256)
         attend_tile(
             start,
             start // 256 + 1,
             True,
-            held[0, rows, :],
+            held[2, rows, :],
             held[3, rows, :],
+            functools.partial(rows_at, 0),
             functools.partial(rows_at, 1),
-            functools.partial(rows_at, 2),
             made.at[0, rows, :],
             made.at[1, rows, :],
             row_codes,
@@ -179,7 +175,7 @@
 
 def split_kernel(
     lag,
-    relay_lag,
+    lead,
     queries,
     keys,
     values,
@@ -194,7 +190,6 @@
     made,
     low_in,
     low_out,
-    stage_in,
     stage_out,
     sums,
     row_codes,
@@ -203,10 +198,13 @@
     values_t,
     keys_sum,
     values_sum,
-    held_recv,
+    pair_recv,
+    rest_recv,
+    outer_recv,
     low_recv,
-    stage_in_recv,
-    stage_out_recv,
+    part_recv,
+    near_recv,
+    stage_recv,
     out_recv,
     send,
     low_send,
@@ -214,17 +212,18 @@
     me = lax.axis_index("seq")
     tokens = queries.shape[0]
     heads = HEADS // 2
+    pair = 2 * tokens
     half = 4 * tokens
     side = lax.rem(me, 2)
     plane = me // 2
     across = me + 1 - 2 * side
-    along = me + 2 - 4 * lax.rem(plane, 2)
-    middle = 6 - 2 * plane + side
-    inner = (plane == 1) | (plane == 2)
-    sources = (queries, keys, values, grads)
+    sources = (keys, values, queries, grads)
     targets = (attended, queries_grad, keys_grad, values_grad)
     scale = 1.0 / math.sqrt(HEAD_DIM)
     scratch = (keys_t, values_t, keys_sum, values_sum)
+
+    def at_plane(z):
+        return 2 * z + side
 
     def columns(which, head):
         return pl.ds(pl.multiple_of((which * heads + head) * HEAD_DIM, HEAD_DIM), HEAD_DIM)
@@ -252,30 +251,210 @@
 
         lax.fori_loop(0, count, step, 0)
 
-    barrier = pltpu.get_barrier_semaphore()
-
-    def greet(device):
-        pl.semaphore_signal(barrier, inc=1, device_id={"seq": device}, device_id_type=MESH)
-
-    def outer_role():
-        greet(across)
-        greet(along)
-        pl.semaphore_wait(barrier, 2)
-
-        def exchange(k):
+    def enter(*others):
+        barrier = pltpu.get_barrier_semaphore()
+        for device in others:
+            pl.semaphore_signal(barrier, inc=1, device_id={"seq": device}, device_id_type=MESH)
+        pl.semaphore_wait(barrier, len(others))
+
+    def arrival(index, k):
+        return pair_recv.at[k] if index < 2 else rest_recv.at[k]
+
+    def exchange(keep):
+        def body(k):
+            for index, source in enumerate(sources):
+                if keep:
+                    pltpu.make_async_copy(
+                        source.at[:, columns(side, k)],
+                        held.at[k, index, rows_of(me), :],
+                        arrival(index, k),
+                    ).start()
+                push(
+                    source.at[:, columns(1 - side, k)],
+                    held.at[k, index, rows_of(me), :],
+                    send.at[0],
+                    arrival(index, k),
+                    across,
+                )
+
+        loop(heads, body)
+
+    def masks(k):
+        build_masks(side * heads + k, lists_ref, dilation_ref, row_codes, key_codes)
+
+    def give_near(index, k):
+        target = targets[index]
+        pltpu.make_async_copy(
+            made.at[k, index, rows_of(me), :], target.at[:, columns(side, k)], out_recv.at[index]
+        ).start()
+        push(
+            made.at[k, index, rows_of(across), :],
+            target.at[:, columns(side, k)],
+            send.at[0],
+            out_recv.at[index],
+            across,
+        )
+
+    def run_ahead(forward, step, finish):
+        for k in range(lead):
+            forward(k)
+
+        def body(k):
+            @pl.when(k + lead < heads)
+            def _():
+                forward(k + lead)
+
+            step(k)
+
+            @pl.when(k >= lag)
+            def _():
+                finish(k - lag)
+
+        loop(heads, body)
+        loop(lag, lambda k: finish(heads - lag + k))
+
+    def add_up(k, rows, extra):
+        for index in range(2):
+            total = sums[k, index] + low_in[k, index, rows, :].astype(jnp.float32)
+            if extra:
+                total = total + low_out[k, index, rows, :].astype(jnp.float32)
+            made[k, 2 + index, rows, :] = (total * (scale if index == 0 else 1.0)).astype(jnp.bfloat16)
+            give_near(2 + index, k)
+
+    def first_role():
+        enter(across, at_plane(1), at_plane(2))
+        exchange(True)
+        rows = slice(0, pair)
+
+        def forward(k):
+            wait_for(held.at[k, pl.ds(0, 2), pl.ds(0, pair), :], pair_recv.at[k])
+            block = held.at[k, pl.ds(0, 2), pl.ds(0, pair), :]
+            push(block, low_in.at[k, :, pl.ds(0, pair), :], send.at[0], low_recv.at[k], at_plane(2))
+            push(block, block, send.at[0], outer_recv.at[k], at_plane(1))
+
+        def step(k):
+            masks(k)
+            wait_for(held.at[k, pl.ds(2, 2), pl.ds(0, pair), :], rest_recv.at[k])
+            attend_rows(
+                [(held.at[k], 0)], [(0, 0)], held.at[k], made.at[k], row_codes, key_codes, scratch
+            )
+            give_near(0, k)
+            give_near(1, k)
+            sums[k, 0] = keys_sum[rows, :]
+            sums[k, 1] = values_sum[rows, :]
+
+        def finish(k):
+            wait_for(low_in.at[k, :, pl.ds(0, pair), :], part_recv.at[k])
+            wait_for(low_out.at[k, :, pl.ds(0, pair), :], near_recv.at[k])
+            add_up(k, rows, True)
+
+        run_ahead(forward, step, finish)
+
+    def second_role():
+        enter(across, at_plane(0), at_plane(2))
+        exchange(True)
+        rows = slice(pair, half)
+
+        def forward(k):
+            block = held.at[k, pl.ds(0, 2), pl.ds(pair, pair), :]
+            wait_for(block, pair_recv.at[k])
+            push(block, low_in.at[k, :, pl.ds(pair, pair), :], send.at[0], low_recv.at[k], at_plane(2))
+
+        def step(k):
+            masks(k)
+            wait_for(held.at[k, pl.ds(2, 2), pl.ds(pair, pair), :], rest_recv.at[k])
+            wait_for(held.at[k, pl.ds(0, 2), pl.ds(0, pair), :], outer_recv.at[k])
+            attend_rows(
+                [(held.at[k], 0), (held.at[k], pair)],
+                [(pair, pair)],
+                held.at[k],
+                made.at[k],
+                row_codes,
+                key_codes,
+                scratch,
+            )
+            low_out[k, 0, :pair, :] = keys_sum[:pair, :].astype(jnp.bfloat16)
+            low_out[k, 1, :pair, :] = values_sum[:pair, :].astype(jnp.bfloat16)
+            block = low_out.at[k, :, pl.ds(0, pair), :]
+            push(block, block, send.at[0], near_recv.at[k], at_plane(0))
+            give_near(0, k)
+            give_near(1, k)
+            sums[k, 0] = keys_sum[rows, :]
+            sums[k, 1] = values_sum[rows, :]
+
+        def finish(k):
+            wait_for(low_in.at[k, :, pl.ds(pair, pair), :], part_recv.at[k])
+            add_up(k, rows, False)
+
+        run_ahead(forward, step, finish)
+
+    def third_role():
+        enter(across, at_plane(0), at_plane(1), at_plane(3))
+        exchange(True)
+
+        def step(k):
+            masks(k)
+            wait_for(held.at[k, pl.ds(0, 2), pl.ds(0, pair), :], pair_recv.at[k])
+            wait_for(held.at[k, pl.ds(2, 2), pl.ds(0, pair), :], rest_recv.at[k])
+            wait_for(held.at[k, :, pl.ds(pair, pair), :], outer_recv.at[k])
+            wait_for(low_in.at[k], low_recv.at[k])
+            attend_rows(
+                [(low_in.at[k], 0), (low_in.at[k], pair), (held.at[k], 0), (held.at[k], pair)],
+                [(0, half), (pair, half + pair)],
+                held.at[k],
+                made.at[k],
+                row_codes,
+                key_codes,
+                scratch,
+            )
+            low_out[k, 0] = keys_sum[:half, :].astype(jnp.bfloat16)
+            low_out[k, 1] = values_sum[:half, :].astype(jnp.bfloat16)
+            for z in range(2):
+                block = pl.ds(z * pair, pair)
+                push(
+                    low_out.at[k, :, block, :],
+                    low_in.at[k, :, block, :],
+                    low_send.at[0],
+                    part_recv.at[k],
+                    at_plane(z),
+                )
+            made[k, 2] = (keys_sum[half:, :] * scale).astype(jnp.bfloat16)
+            made[k, 3] = values_sum[half:, :].astype(jnp.bfloat16)
+            along = at_plane(3)
+            far = rows_of(along + 1 - 2 * side)
+            for index, target in enumerate(targets):
+                push(made.at[k, index, far, :], stage_out.at[k, index], send.at[0], stage_recv.at[k], along)
+                push(
+                    made.at[k, index, rows_of(along), :],
+                    target.at[:, columns(side, k)],
+                    send.at[0],
+                    out_recv.at[index],
+                    along,
+                )
+                give_near(index, k)
+
+        loop(heads, step)
+
+    def fourth_role():
+        enter(across, at_plane(2))
+        exchange(False)
+
+        def forward(k):
             for index, source in enumerate(sources):
                 push(
-                    source.at[:, columns(1 - side, k)],
-                    stage_in.at[k, index],
+                    source.at[:, columns(side, k)],
+                    held.at[k, index, rows_of(me), :],
                     send.at[0],
-                    stage_in_recv.at[k],
-                    across,
+                    outer_recv.at[k],
+                    at_plane(2),
                 )
-
-        loop(heads, exchange)
-
-        def relay_out(k):
-            wait_for(stage_out.at[k], stage_out_recv.at[k])
+            for first, sem in ((0, pair_recv), (2, rest_recv)):
+                block = held.at[k, pl.ds(first, 2), rows_of(across), :]
+                wait_for(block, sem.at[k])
+                push(block, block, send.at[0], outer_recv.at[k], at_plane(2))
+
+        def finish(k):
+            wait_for(stage_out.at[k], stage_recv.at[k])
             for index, target in enumerate(targets):
                 push(
                     stage_out.at[k, index],
@@ -285,133 +464,56 @@
                     across,
                 )
 
-        def relay_in(k):
-            for index, source in enumerate(sources):
-                push(
-                    source.at[:, columns(side, k)],
-                    held.at[k, index, rows_of(me), :],
-                    send.at[0],
-                    held_recv.at[k],
-                    along,
-                )
-            wait_for(stage_in.at[k], stage_in_recv.at[k])
-            for index in range(4):
-                push(
-                    stage_in.at[k, index],
-                    held.at[k, index, rows_of(across), :],
-                    send.at[0],
-                    held_recv.at[k],
-                    along,
-                )
-
-        def both(k):
-            relay_in(k)
-
-            @pl.when(k >= relay_lag)
-            def _():
-                relay_out(k - relay_lag)
-
-        loop(heads, both)
-        loop(relay_lag, lambda k: relay_out(heads - relay_lag + k))
-
-    def give(index, k):
-        target = targets[index]
-        far = rows_of(along + across - me)
-        pltpu.make_async_copy(
-            made.at[k, index, rows_of(me), :], target.at[:, columns(side, k)], out_recv.at[index]
-        ).start()
-        push(made.at[k, index, far, :], stage_out.at[k, index], send.at[0], stage_out_recv.at[k], along)
-        push(
-            made.at[k, index, rows_of(along), :],
-            target.at[:, columns(side, k)],
-            send.at[0],
-            out_recv.at[index],
-            along,
-        )
-        push(
-            made.at[k, index, rows_of(across), :],
-            target.at[:, columns(side, k)],
-            send.at[0],
-            out_recv.at[index],
-            across,
-        )
-
-    def inner_start():
-        greet(across)
-        greet(along)
-        greet(middle)
-        pl.semaphore_wait(barrier, 3)
-
-        def exchange(k):
-            for index, source in enumerate(sources):
-                pltpu.make_async_copy(
-                    source.at[:, columns(side, k)],
-                    held.at[k, index, rows_of(me), :],
-                    held_recv.at[k],
-                ).start()
-                push(
-                    source.at[:, columns(1 - side, k)],
-                    held.at[k, index, rows_of(me), :],
-                    send.at[0],
-                    held_recv.at[k],
-                    across,
-                )
-
-        loop(heads, exchange)
-
-    def lower_role():
-        inner_start()
-
-        def finish(k):
-            wait_for(low_in.at[k], low_recv.at[k])
-            made[k, 2] = ((sums[k, 0] + low_in[k, 0].astype(jnp.float32)) * scale).astype(jnp.bfloat16)
-            made[k, 3] = (sums[k, 1] + low_in[k, 1].astype(jnp.float32)).astype(jnp.bfloat16)
-            give(2, k)
-            give(3, k)
-
-        def step(k):
-            build_masks(side * heads + k, lists_ref, dilation_ref, row_codes, key_codes)
-            wait_for(held.at[k], held_recv.at[k])
-            push(held.at[k, pl.ds(1, 2)], low_in.at[k], low_send.at[0], low_recv.at[k], middle)
-            attend_half(False, held.at[k], None, made.at[k], row_codes, key_codes, scratch)
-            give(0, k)
-            give(1, k)
-            sums[k, 0] = keys_sum[:half, :]
-            sums[k, 1] = values_sum[:half, :]
-
-            @pl.when(k >= lag)
-            def _():
-                finish(k - lag)
-
-        loop(heads, step)
-        loop(lag, lambda k: finish(heads - lag + k))
-
-    def upper_role():
-        inner_start()
-
-        def step(k):
-            build_masks(side * heads + k, lists_ref, dilation_ref, row_codes, key_codes)
-            wait_for(held.at[k], held_recv.at[k])
-            wait_for(low_in.at[k], low_recv.at[k])
-            attend_half(True, held.at[k], low_in.at[k], made.at[k], row_codes, key_codes, scratch)
-            low_out[k, 0] = keys_sum[:half, :].astype(jnp.bfloat16)
-            low_out[k, 1] = values_sum[:half, :].astype(jnp.bfloat16)
-            push(low_out.at[k], low_in.at[k], low_send.at[0], low_recv.at[k], middle)
-            made[k, 2] = (keys_sum[half:, :] * scale).astype(jnp.bfloat16)
-            made[k, 3] = values_sum[half:, :].astype(jnp.bfloat16)
-            for index in range(4):
-                give(index, k)
-
-        loop(heads, step)
-
-    pl.when(jnp.logical_not(inner))(outer_role)
-    pl.when(plane == 1)(lower_role)
-    pl.when(plane == 2)(upper_role)
+        run_ahead(forward, lambda k: None, finish)
+
+    for z, role in enumerate((first_role, second_role, third_role, fourth_role)):
+        pl.when(plane == z)(role)
 
     wait_for(held, send.at[0])
-    pl.when(inner)(lambda: wait_for(low_in, low_send.at[0]))
+    pl.when(plane == 2)(lambda: wait_for(low_in, low_send.at[0]))
     for index, target in enumerate(targets):
         wait_for(target, out_recv.at[index])
+
+
+def settle_kernel(pieces, *refs):
+    sources, targets, slots, load, store = refs[:4], refs[4:8], refs[8], refs[9], refs[10]
+    rows = sources[0].shape[0] // pieces
+    loads, stores = [], []
+    for index in range(4):
+        for piece in range(pieces):
+            span = pl.ds(piece * rows, rows)
+            number = index * pieces + piece
+            loads.append(
+                pltpu.make_async_copy(sources[index].at[span, :], slots.at[index, span, :], load.at[number])
+            )
+            stores.append(
+                pltpu.make_async_copy(slots.at[index, span, :], targets[index].at[span, :], store.at[number])
+            )
+    for copy in loads:
+        copy.start()
+    for arrived, copy in zip(loads, stores):
+        arrived.wait()
+        copy.start()
+    for copy in stores:
+        copy.wait()
+
+
+def settle(arrays):
+    rows, width = arrays[0].shape
+    pieces = 4
+    anywhere = pl.BlockSpec(memory_space=pl.ANY)
+    return pl.pallas_call(
+        functools.partial(settle_kernel, pieces),
+        out_shape=(jax.ShapeDtypeStruct((rows, width), jnp.bfloat16),) * 4,
+        in_specs=[anywhere] * 4,
+        out_specs=(anywhere,) * 4,
+        scratch_shapes=[
+            pltpu.VMEM((4, rows, width), jnp.bfloat16),
+            pltpu.SemaphoreType.DMA((4 * pieces,)),
+            pltpu.SemaphoreType.DMA((4 * pieces,)),
+        ],
+        compiler_params=pltpu.CompilerParams(vmem_limit_bytes=56 * 1024 * 1024),
+    )(*arrays)
 
 
 def kernel(
@@ -546,23 +648,19 @@
         pltpu.VMEM((seq, HEAD_DIM), jnp.float32),
         pltpu.VMEM((seq, HEAD_DIM), jnp.float32),
     ]
-    if n == 8 and tokens % 64 == 0:
+    if n == 8 and tokens == 128:
         heads = HEADS // 2
         half = seq // 2
-        body = functools.partial(split_kernel, 5, 8)
+        body = functools.partial(split_kernel, 8, 2)
         scratch = [
             pltpu.VMEM((heads, 4, half, HEAD_DIM), jnp.bfloat16),
             pltpu.VMEM((heads, 4, half, HEAD_DIM), jnp.bfloat16),
             pltpu.VMEM((heads, 2, half, HEAD_DIM), jnp.bfloat16),
             pltpu.VMEM((heads, 2, half, HEAD_DIM), jnp.bfloat16),
             pltpu.VMEM((heads, 4, tokens, HEAD_DIM), jnp.bfloat16),
-            pltpu.VMEM((heads, 4, tokens, HEAD_DIM), jnp.bfloat16),
-            pltpu.VMEM((heads, 2, half, HEAD_DIM), jnp.float32),
+            pltpu.VMEM((heads, 2, 2 * tokens, HEAD_DIM), jnp.float32),
             *work,
-            pltpu.SemaphoreType.DMA((heads,)),
-            pltpu.SemaphoreType.DMA((heads,)),
-            pltpu.SemaphoreType.DMA((heads,)),
-            pltpu.SemaphoreType.DMA((heads,)),
+            *[pltpu.SemaphoreType.DMA((heads,))] * 7,
             pltpu.SemaphoreType.DMA((4,)),
             pltpu.SemaphoreType.DMA((1,)),
             pltpu.SemaphoreType.DMA((1,)),
@@ -579,7 +677,7 @@
             pltpu.SemaphoreType.DMA((heads,)),
             pltpu.SemaphoreType.DMA((4,)),
         ]
-    return pl.pallas_call(
+    results = pl.pallas_call(
         body,
         out_shape=(row,) * 4,
         in_specs=[anywhere] * 4
@@ -589,7 +687,8 @@
         compiler_params=pltpu.CompilerParams(
             collective_id=0, has_side_effects=True, vmem_limit_bytes=56 * 1024 * 1024
         ),
-    )(queries, keys, values, out_grad, key_blocks, dilation)
+    )(queries, keys, values, out_grad, jnp.transpose(key_blocks, (2, 1, 0)), dilation)
+    return settle(results)
 
 
 def solution(mesh):

time: 134 us -> 119 us (0.89)
  local copies, waits for them, and re-layouts: 8.33 us -> 0 us
  Pallas kernels: 124 us -> 117 us
    pallas_call x1, Pallas kernels: 124 us -> 114 us  [local(): pl.pallas_call(body, out_shape=(row,) * 4, in_specs=[anywhere] * 4 + [pl....]
    unnamed x11 -> x0, local copies, waits for them, and re-layouts: 8.33 us -> none
    pallas_call x0 -> x1, Pallas kernels: none -> 3.85 us  [settle(): pl.pallas_call(functools.partial(settle_kernel, pieces), out_shape=(jax.S...]
where the time goes in v3:
time: 119 us; the launch traced here: 118 us
  Pallas kernels  117 us (98%)
    pallas_call x1, Pallas kernels, local(): pl.pallas_call(body, out_shape=(row,) * 4, in_specs=[anywhere] * 4 + [pl....  114 us
    pallas_call x1, Pallas kernels, settle(): pl.pallas_call(functools.partial(settle_kernel, pieces), out_shape=(jax.S...  3.85 us

profile of v3, /device:TPU:0, one launch (start us, length us, event | category | flops | bytes accessed | tf_op | source)
XLA Modules:
  0.0 118.0 jit_solution(3528048866312578256)
XLA Ops:
  0.6 113.6 %shard_map.93 = (bf16[128,4096]{1,0:T(8,128)(2,1)}, bf16[128,4096]{1,0:T(8,128)(2,1)}, bf16[128,4096]{1,0:T(8,128)(2,1)}, bf16[128,4096]{1,0:T(8,128)(2,1)}) custom-call(bf16[128,4096]{1,0:T(8,128)(2,1)} %queries.1, bf16[128,4096]{1,0:T(8,128)(2,1)} %keys.1, bf16[128,4096]{1,0:T(8,128)(2,1)} %values.1, bf16[128,4096]{1,0:T(8,128)(2,1)} %grads.1, ...), custom_call_target="tpu_custom_call" | custom-call | tf_op jit(solution)/shard_map/pallas_call | solution.py:680
  114.2 3.9 %shard_map.94 = (bf16[128,4096]{1,0:T(8,128)(2,1)}, bf16[128,4096]{1,0:T(8,128)(2,1)}, bf16[128,4096]{1,0:T(8,128)(2,1)}, bf16[128,4096]{1,0:T(8,128)(2,1)}) custom-call(bf16[128,4096]{1,0:T(8,128)(2,1)} %get-tuple-element.8.refs_0_, bf16[128,4096]{1,0:T(8,128)(2,1)} %get-tuple-element.9.refs_1_, bf16[128,4096]{1,0:T(8,128)(2,1)} %get-tuple-element.10.refs_2_, ...), custom_call_target="tpu_custom_call" | custom-call | tf_op jit(solution)/shard_map/pallas_call | solution.py:505

commit v4 on v3

--- a/solution.py
+++ b/solution.py
@@ -260,24 +260,21 @@
     def arrival(index, k):
         return pair_recv.at[k] if index < 2 else rest_recv.at[k]
 
-    def exchange(keep):
-        def body(k):
-            for index, source in enumerate(sources):
-                if keep:
-                    pltpu.make_async_copy(
-                        source.at[:, columns(side, k)],
-                        held.at[k, index, rows_of(me), :],
-                        arrival(index, k),
-                    ).start()
-                push(
-                    source.at[:, columns(1 - side, k)],
+    def exchange(k, keep=True):
+        for index, source in enumerate(sources):
+            if keep:
+                pltpu.make_async_copy(
+                    source.at[:, columns(side, k)],
                     held.at[k, index, rows_of(me), :],
-                    send.at[0],
                     arrival(index, k),
-                    across,
-                )
-
-        loop(heads, body)
+                ).start()
+            push(
+                source.at[:, columns(1 - side, k)],
+                held.at[k, index, rows_of(me), :],
+                send.at[0],
+                arrival(index, k),
+                across,
+            )
 
     def masks(k):
         build_masks(side * heads + k, lists_ref, dilation_ref, row_codes, key_codes)
@@ -295,23 +292,24 @@
             across,
         )
 
-    def run_ahead(forward, step, finish):
-        for k in range(lead):
-            forward(k)
-
-        def body(k):
-            @pl.when(k + lead < heads)
-            def _():
-                forward(k + lead)
-
-            step(k)
-
-            @pl.when(k >= lag)
-            def _():
-                finish(k - lag)
-
-        loop(heads, body)
-        loop(lag, lambda k: finish(heads - lag + k))
+    def run_ahead(stages):
+        for lead, body in stages:
+            if lead > 0:
+                loop(lead, body)
+
+        def step(k):
+            for lead, body in stages:
+                if lead > 0:
+                    pl.when(k + lead < heads)(functools.partial(body, k + lead))
+                elif lead < 0:
+                    pl.when(k + lead >= 0)(functools.partial(body, k + lead))
+                else:
+                    body(k)
+
+        loop(heads, step)
+        for lead, body in stages:
+            if lead < 0:
+                loop(-lead, lambda k, lead=lead, body=body: body(heads + lead + k))
 
     def add_up(k, rows, extra):
         for index in range(2):
@@ -323,7 +321,6 @@
 
     def first_role():
         enter(across, at_plane(1), at_plane(2))
-        exchange(True)
         rows = slice(0, pair)
 
         def forward(k):
@@ -348,11 +345,10 @@
             wait_for(low_out.at[k, :, pl.ds(0, pair), :], near_recv.at[k])
             add_up(k, rows, True)
 
-        run_ahead(forward, step, finish)
+        run_ahead([(2 * lead, exchange), (lead, forward), (0, step), (-lag, finish)])
 
     def second_role():
         enter(across, at_plane(0), at_plane(2))
-        exchange(True)
         rows = slice(pair, half)
 
         def forward(k):
@@ -386,11 +382,10 @@
             wait_for(low_in.at[k, :, pl.ds(pair, pair), :], part_recv.at[k])
             add_up(k, rows, False)
 
-        run_ahead(forward, step, finish)
+        run_ahead([(2 * lead, exchange), (lead, forward), (0, step), (-lag, finish)])
 
     def third_role():
         enter(across, at_plane(0), at_plane(1), at_plane(3))
-        exchange(True)
 
         def step(k):
             masks(k)
@@ -422,8 +417,9 @@
             made[k, 3] = values_sum[half:, :].astype(jnp.bfloat16)
             along = at_plane(3)
             far = rows_of(along + 1 - 2 * side)
+            for index in range(4):
+                push(made.at[k, index, far, :], stage_out.at[k, index], send.at[0], stage_recv.at[k], along)
             for index, target in enumerate(targets):
-                push(made.at[k, index, far, :], stage_out.at[k, index], send.at[0], stage_recv.at[k], along)
                 push(
                     made.at[k, index, rows_of(along), :],
                     target.at[:, columns(side, k)],
@@ -433,13 +429,12 @@
                 )
                 give_near(index, k)
 
-        loop(heads, step)
+        run_ahead([(2 * lead, exchange), (0, step)])
 
     def fourth_role():
         enter(across, at_plane(2))
-        exchange(False)
-
-        def forward(k):
+
+        def own(k):
             for index, source in enumerate(sources):
                 push(
                     source.at[:, columns(side, k)],
@@ -448,6 +443,8 @@
                     outer_recv.at[k],
                     at_plane(2),
                 )
+
+        def forward(k):
             for first, sem in ((0, pair_recv), (2, rest_recv)):
                 block = held.at[k, pl.ds(first, 2), rows_of(across), :]
                 wait_for(block, sem.at[k])
@@ -464,7 +461,14 @@
                     across,
                 )
 
-        run_ahead(forward, lambda k: None, finish)
+        run_ahead(
+            [
+                (2 * lead, functools.partial(exchange, keep=False)),
+                (lead, own),
+                (0, forward),
+                (-lag, finish),
+            ]
+        )
 
     for z, role in enumerate((first_role, second_role, third_role, fourth_role)):
         pl.when(plane == z)(role)

time: 119 us -> 121 us (1.017)
  Pallas kernels: 117 us -> 120 us
    pallas_call x1, Pallas kernels: 114 us -> 116 us  [local(): pl.pallas_call(body, out_shape=(row,) * 4, in_specs=[anywhere] * 4 + [pl....]
where the time goes in v4:
time: 121 us
  Pallas kernels  120 us (99%)
    pallas_call x1, Pallas kernels, local(): pl.pallas_call(body, out_shape=(row,) * 4, in_specs=[anywhere] * 4 + [pl....  116 us
    pallas_call x1, Pallas kernels, settle(): pl.pallas_call(functools.partial(settle_kernel, pieces), out_shape=(jax.S...  3.85 us

profile of v4, /device:TPU:0, one launch (start us, length us, event | category | flops | bytes accessed | tf_op | source)
XLA Modules:
  0.0 120.6 jit_solution(14939099239145726231)
XLA Ops:
  0.6 116.1 %shard_map.93 = (bf16[128,4096]{1,0:T(8,128)(2,1)}, bf16[128,4096]{1,0:T(8,128)(2,1)}, bf16[128,4096]{1,0:T(8,128)(2,1)}, bf16[128,4096]{1,0:T(8,128)(2,1)}) custom-call(bf16[128,4096]{1,0:T(8,128)(2,1)} %queries.1, bf16[128,4096]{1,0:T(8,128)(2,1)} %keys.1, bf16[128,4096]{1,0:T(8,128)(2,1)} %values.1, bf16[128,4096]{1,0:T(8,128)(2,1)} %grads.1, ...), custom_call_target="tpu_custom_call" | custom-call | tf_op jit(solution)/shard_map/pallas_call | solution.py:684
  116.7 3.9 %shard_map.94 = (bf16[128,4096]{1,0:T(8,128)(2,1)}, bf16[128,4096]{1,0:T(8,128)(2,1)}, bf16[128,4096]{1,0:T(8,128)(2,1)}, bf16[128,4096]{1,0:T(8,128)(2,1)}) custom-call(bf16[128,4096]{1,0:T(8,128)(2,1)} %get-tuple-element.8.refs_0_, bf16[128,4096]{1,0:T(8,128)(2,1)} %get-tuple-element.9.refs_1_, bf16[128,4096]{1,0:T(8,128)(2,1)} %get-tuple-element.10.refs_2_, ...), custom_call_target="tpu_custom_call" | custom-call | tf_op jit(solution)/shard_map/pallas_call | solution.py:509

commit v5 on v4

--- a/solution.py
+++ b/solution.py
@@ -52,7 +52,7 @@
 
 
 def attend_tile(
-    start, chunks, diagonal_only, query, grad, key_at, value_at, attended, queries_grad, row_codes, key_codes, scratch
+    start, chunks, diagonal_only, fresh, query, grad, key_at, value_at, attended, queries_grad, row_codes, key_codes, scratch
 ):
     keys_t, values_t, keys_sum, values_sum = scratch
     scale = 1.0 / math.sqrt(HEAD_DIM)
@@ -80,32 +80,42 @@
             seen = seen & (key_ids <= query_ids)
         scores.append(jnp.where(seen, raw, very_low / scale))
     top = functools.reduce(jnp.maximum, [jnp.max(s, axis=0, keepdims=True) for s in scores])
-    expos = [jnp.exp2((s - top) * (scale * math.log2(math.e))) for s in scores]
+    yield
+    expos, dweights = [], []
+    for c in range(chunks):
+        dweights.append(dot(value_at(c), grad, LAST))
+        expos.append(jnp.exp2((scores[c] - top) * (scale * math.log2(math.e))))
     total = sum(jnp.sum(e, axis=0, keepdims=True) for e in expos)
     share = 1.0 / total
-    weights = [e * share for e in expos]
-    weights16 = [w.astype(jnp.bfloat16) for w in weights]
-    out_t = sum(
-        dot(values_t[:, c * chunk : (c + 1) * chunk], weights16[c], PLAIN) for c in range(chunks)
-    )
-    out16 = jnp.transpose(out_t).astype(jnp.bfloat16)
-    attended[...] = out16
-    product_t = jnp.transpose(grad.astype(jnp.float32) * out16.astype(jnp.float32))
-    delta = jnp.sum(product_t, axis=0, keepdims=True)
+    grad_t = turned(grad).astype(jnp.float32)
+    yield
+    weights, out_t = [], None
+    for c in range(chunks):
+        span = slice(c * chunk, (c + 1) * chunk)
+        weights.append(expos[c] * share)
+        weights16 = weights[c].astype(jnp.bfloat16)
+        part = dot(values_t[:, span], weights16, PLAIN)
+        out_t = part if out_t is None else out_t + part
+        part = dot(weights16, grad, PLAIN)
+        values_sum[span, :] = part if fresh else values_sum[span, :] + part
+    out16_t = out_t.astype(jnp.bfloat16)
+    attended[...] = jnp.transpose(out16_t)
+    delta = jnp.sum(grad_t * out16_t.astype(jnp.float32), axis=0, keepdims=True)
+    yield
     query_t = None
     for c in range(chunks):
         span = slice(c * chunk, (c + 1) * chunk)
-        values_sum[span, :] += dot(weights16[c], grad, PLAIN)
-        dweights = dot(value_at(c), grad, LAST)
-        dscores16 = (weights[c] * (dweights - delta)).astype(jnp.bfloat16)
-        keys_sum[span, :] += dot(dscores16, query, PLAIN)
+        dscores16 = (weights[c] * (dweights[c] - delta)).astype(jnp.bfloat16)
+        part = dot(dscores16, query, PLAIN)
+        keys_sum[span, :] = part if fresh else keys_sum[span, :] + part
         part = dot(keys_t[:, span], dscores16, PLAIN)
         query_t = part if query_t is None else query_t + part
-    queries_grad[...] = jnp.transpose(query_t * scale).astype(jnp.bfloat16)
+    queries_grad[...] = jnp.transpose((query_t * scale).astype(jnp.bfloat16))
+    yield
 
 
 def turned(rows):
-    return jnp.transpose(rows.astype(jnp.float32)).astype(jnp.bfloat16)
+    return jnp.transpose(rows)
 
 
 def attend_head(ins, outs, row_codes, key_codes, scratch):
@@ -121,9 +131,10 @@
     def one(index, carry):
         start = pl.multiple_of(index * 128, 128)
         rows = pl.ds(start, 128)
-        attend_tile(
+        phases = attend_tile(
             start,
             seq // 256,
+            False,
             False,
             queries[rows, :],
             grads[rows, :],
@@ -135,6 +146,8 @@
             key_codes,
             scratch,
         )
+        for _ in phases:
+            pass
         return carry
 
     lax.fori_loop(0, seq // 128, one, 0)
@@ -153,14 +166,14 @@
         span = slice(c * 256, (c + 1) * 256)
         keys_t[:, span] = turned(rows_at(0, c))
         values_t[:, span] = turned(rows_at(1, c))
-        keys_sum[span, :] = jnp.zeros((256, HEAD_DIM), jnp.float32)
-        values_sum[span, :] = jnp.zeros((256, HEAD_DIM), jnp.float32)
-    for first, start in query_tiles:
+    tiles = []
+    for number, (first, start) in enumerate(query_tiles):
         rows = slice(first, first + 256)
-        attend_tile(
+        phases = attend_tile(
             start,
             start // 256 + 1,
             True,
+            number == 0,
             held[2, rows, :],
             held[3, rows, :],
             functools.partial(rows_at, 0),
@@ -171,6 +184,9 @@
             key_codes,
             scratch,
         )
+        tiles.append(phases)
+    for _ in zip(*tiles):
+        pass
 
 
 def split_kernel(
@@ -395,7 +411,7 @@
             wait_for(low_in.at[k], low_recv.at[k])
             attend_rows(
                 [(low_in.at[k], 0), (low_in.at[k], pair), (held.at[k], 0), (held.at[k], pair)],
-                [(0, half), (pair, half + pair)],
+                [(pair, half + pair), (0, half)],
                 held.at[k],
                 made.at[k],
                 row_codes,

time: 121 us -> 119 us (0.983)
    pallas_call x1, Pallas kernels: 116 us -> 115 us  [local(): pl.pallas_call(body, out_shape=(row,) * 4, in_specs=[anywhere] * 4 + [pl....]
where the time goes in v5:
time: 119 us
  Pallas kernels  119 us (100%)
    pallas_call x1, Pallas kernels, local(): pl.pallas_call(body, out_shape=(row,) * 4, in_specs=[anywhere] * 4 + [pl....  115 us
    pallas_call x1, Pallas kernels, settle(): pl.pallas_call(functools.partial(settle_kernel, pieces), out_shape=(jax.S...  3.85 us

profile of v5, /device:TPU:0, one launch (start us, length us, event | category | flops | bytes accessed | tf_op | source)
XLA Modules:
  0.0 119.3 jit_solution(16217082246681844064)
XLA Ops:
  0.6 114.8 %shard_map.93 = (bf16[128,4096]{1,0:T(8,128)(2,1)}, bf16[128,4096]{1,0:T(8,128)(2,1)}, bf16[128,4096]{1,0:T(8,128)(2,1)}, bf16[128,4096]{1,0:T(8,128)(2,1)}) custom-call(bf16[128,4096]{1,0:T(8,128)(2,1)} %queries.1, bf16[128,4096]{1,0:T(8,128)(2,1)} %keys.1, bf16[128,4096]{1,0:T(8,128)(2,1)} %values.1, bf16[128,4096]{1,0:T(8,128)(2,1)} %grads.1, ...), custom_call_target="tpu_custom_call" | custom-call | tf_op jit(solution)/shard_map/pallas_call | solution.py:700
  115.4 3.9 %shard_map.94 = (bf16[128,4096]{1,0:T(8,128)(2,1)}, bf16[128,4096]{1,0:T(8,128)(2,1)}, bf16[128,4096]{1,0:T(8,128)(2,1)}, bf16[128,4096]{1,0:T(8,128)(2,1)}) custom-call(bf16[128,4096]{1,0:T(8,128)(2,1)} %get-tuple-element.8.refs_0_, bf16[128,4096]{1,0:T(8,128)(2,1)} %get-tuple-element.9.refs_1_, bf16[128,4096]{1,0:T(8,128)(2,1)} %get-tuple-element.10.refs_2_, ...), custom_call_target="tpu_custom_call" | custom-call | tf_op jit(solution)/shard_map/pallas_call | solution.py:525

commit v6 on v5

--- a/solution.py
+++ b/solution.py
@@ -433,8 +433,7 @@
             made[k, 3] = values_sum[half:, :].astype(jnp.bfloat16)
             along = at_plane(3)
             far = rows_of(along + 1 - 2 * side)
-            for index in range(4):
-                push(made.at[k, index, far, :], stage_out.at[k, index], send.at[0], stage_recv.at[k], along)
+            push(made.at[k, :, far, :], stage_out.at[k], send.at[0], stage_recv.at[k], along)
             for index, target in enumerate(targets):
                 push(
                     made.at[k, index, rows_of(along), :],
@@ -477,14 +476,18 @@
                     across,
                 )
 
-        run_ahead(
-            [
-                (2 * lead, functools.partial(exchange, keep=False)),
-                (lead, own),
-                (0, forward),
-                (-lag, finish),
-            ]
-        )
+        exchange(0, False)
+        own(0)
+        loop(2 * lead - 1, lambda k: exchange(k + 1, False))
+
+        def step(k):
+            forward(k)
+            pl.when(k + 1 < heads)(lambda: own(k + 1))
+            pl.when(k + 2 * lead < heads)(lambda: exchange(k + 2 * lead, False))
+            pl.when(k >= lag)(lambda: finish(k - lag))
+
+        loop(heads, step)
+        loop(lag, lambda k: finish(heads - lag + k))
 
     for z, role in enumerate((first_role, second_role, third_role, fourth_role)):
         pl.when(plane == z)(role)

time: 119 us -> 119 us (level); the launches traced: 119 us -> 117 us
  Pallas kernels: 119 us -> 117 us
    pallas_call x1, Pallas kernels: 115 us -> 113 us  [local(): pl.pallas_call(body, out_shape=(row,) * 4, in_specs=[anywhere] * 4 + [pl....]
where the time goes in v6:
time: 119 us; the launch traced here: 117 us
  Pallas kernels  117 us (98%)
    pallas_call x1, Pallas kernels, local(): pl.pallas_call(body, out_shape=(row,) * 4, in_specs=[anywhere] * 4 + [pl....  113 us
    pallas_call x1, Pallas kernels, settle(): pl.pallas_call(functools.partial(settle_kernel, pieces), out_shape=(jax.S...  3.85 us

profile of v6, /device:TPU:0, one launch (start us, length us, event | category | flops | bytes accessed | tf_op | source)
XLA Modules:
  0.0 117.3 jit_solution(4511761257561594099)
XLA Ops:
  0.6 112.8 %shard_map.93 = (bf16[128,4096]{1,0:T(8,128)(2,1)}, bf16[128,4096]{1,0:T(8,128)(2,1)}, bf16[128,4096]{1,0:T(8,128)(2,1)}, bf16[128,4096]{1,0:T(8,128)(2,1)}) custom-call(bf16[128,4096]{1,0:T(8,128)(2,1)} %queries.1, bf16[128,4096]{1,0:T(8,128)(2,1)} %keys.1, bf16[128,4096]{1,0:T(8,128)(2,1)} %values.1, bf16[128,4096]{1,0:T(8,128)(2,1)} %grads.1, ...), custom_call_target="tpu_custom_call" | custom-call | tf_op jit(solution)/shard_map/pallas_call | solution.py:703
  113.4 3.9 %shard_map.94 = (bf16[128,4096]{1,0:T(8,128)(2,1)}, bf16[128,4096]{1,0:T(8,128)(2,1)}, bf16[128,4096]{1,0:T(8,128)(2,1)}, bf16[128,4096]{1,0:T(8,128)(2,1)}) custom-call(bf16[128,4096]{1,0:T(8,128)(2,1)} %get-tuple-element.8.refs_0_, bf16[128,4096]{1,0:T(8,128)(2,1)} %get-tuple-element.9.refs_1_, bf16[128,4096]{1,0:T(8,128)(2,1)} %get-tuple-element.10.refs_2_, ...), custom_call_target="tpu_custom_call" | custom-call | tf_op jit(solution)/shard_map/pallas_call | solution.py:528
